TPU v7x, 32 devices: a whole 2x2x4 slice. The times are simulated.
32 devices in a mesh: dp: 4 (over y, core), seq: 8 (over z, x).
Axes of the slice: x: 2, y: 2, z: 4, core: 2. Of those that a mesh axis runs over, the one named last changes fastest.
Arguments:
- inputs: bfloat16 [20480, 512], P(('dp', 'seq')), may hold values from -6 to 6
- cotangent: bfloat16 [20480, 512], P(('dp', 'seq')), may hold values from -6 to 6
- block_segment: int32 [160], P('dp'), may hold values from 0 to 39, as said below
- segment_parent: int32 [160], P('dp'), may hold values from -1 to 39, as said below
- query_weight: bfloat16 [512, 512], P(('dp', 'seq')), may hold values from -0.5 to 0.5
- key_weight: bfloat16 [512, 512], P(('dp', 'seq')), may hold values from -0.25 to 0.25
- value_weight: bfloat16 [512, 512], P(('dp', 'seq')), may hold values from -0.25 to 0.25
- output_weight: bfloat16 [512, 512], P(('dp', 'seq')), may hold values from -1 to 1
- gate_weight: bfloat16 [512, 512], P(('dp', 'seq')), may hold values from -0.25 to 0.25
- gate_bias: bfloat16 [512], P(('dp', 'seq')), may hold values from -3 to 3
- up_weight: bfloat16 [512, 2048], P(('dp', 'seq')), may hold values from -0.25 to 0.25
- up_bias: bfloat16 [2048], P(('dp', 'seq')), may hold values from -3 to 3
- down_weight: bfloat16 [2048, 512], P(('dp', 'seq')), may hold values from -0.125 to 0.125
- down_bias: bfloat16 [512], P(('dp', 'seq')), may hold values from -3 to 3
- carry_weight: bfloat16 [512, 512], P(('dp', 'seq')), may hold values from -0.25 to 0.25
- carry_bias: bfloat16 [512], P(('dp', 'seq')), may hold values from -3 to 3
- first_gain: bfloat16 [512], P(('dp', 'seq')), may hold values from 0.25 to 1.75
- first_shift: bfloat16 [512], P(('dp', 'seq')), may hold values from -2 to 2
- second_gain: bfloat16 [512], P(('dp', 'seq')), may hold values from 0.25 to 1.75
- second_shift: bfloat16 [512], P(('dp', 'seq')), may hold values from -2 to 2
Outputs:
- output: bfloat16 [20480, 512], P(('dp', 'seq'))
- input_grad: float32 [20480, 512], P(('dp', 'seq'))
- query_weight_grad: float32 [512, 512], P(('dp', 'seq'))
- key_weight_grad: float32 [512, 512], P(('dp', 'seq'))
- value_weight_grad: float32 [512, 512], P(('dp', 'seq'))
- output_weight_grad: float32 [512, 512], P(('dp', 'seq'))
- gate_weight_grad: float32 [512, 512], P(('dp', 'seq'))
- gate_bias_grad: float32 [512], P(('dp', 'seq'))
- up_weight_grad: float32 [512, 2048], P(('dp', 'seq'))
- up_bias_grad: float32 [2048], P(('dp', 'seq'))
- down_weight_grad: float32 [2048, 512], P(('dp', 'seq'))
- down_bias_grad: float32 [512], P(('dp', 'seq'))
- carry_weight_grad: float32 [512, 512], P(('dp', 'seq'))
- carry_bias_grad: float32 [512], P(('dp', 'seq'))
- first_gain_grad: float32 [512], P(('dp', 'seq'))
- first_shift_grad: float32 [512], P(('dp', 'seq'))
- second_gain_grad: float32 [512], P(('dp', 'seq'))
- second_shift_grad: float32 [512], P(('dp', 'seq'))
Inputs may be any that keep to these rules, and one draw needn't show every extreme that they name: `segment_parent`: entry s of a dp group's 40 entries is the parent of segment s of that group, or -1 for a root. The group's segments form 2 trees of 20 segments: a chain of 8 from the root, 4 children of the chain's last segment, and 2 children of each of those. `block_segment`: each dp group's 40 entries are a permutation of its segment numbers; entry j names the segment held in slot j, on the device of index j // 5 along seq.
All inputs are finite; a program needn't handle non-finite values.
Results may differ from a plain program's by a relative error of at most 0.035.
Values may be sent and summed in bfloat16 or wider, within the bound.
No kernel may reach another device: no remote copies, remote signals or barrier semaphores. Data moves between devices by JAX's collectives and lax.ppermute only.
A program may use at most 256 MiB of HBM per device.

v0:
```python
import jax
import jax.numpy as jnp
from jax import lax
from jax.sharding import PartitionSpec as P

HD = 64
BLK = 128
DEPTH = 10


EPSILON = 1e-05
NEGATIVE = -1e30


def normalize(values, norm_gain, norm_shift):
    center = values - jnp.mean(values, axis=-1, keepdims=True)
    spread = jnp.mean(center * center, axis=-1, keepdims=True)
    return center * lax.rsqrt(spread + EPSILON) * norm_gain + norm_shift


def matmul(left_side, right_side):
    return jnp.dot(left_side, right_side, preferred_element_type=jnp.float32)


def inner_rows(left_side, right_side):
    return lax.dot_general(
        left_side, right_side, (((0,), (0,)), ((), ())), preferred_element_type=jnp.float32
    )


def against(left_side, right_side):
    return lax.dot_general(
        left_side, right_side, (((1,), (1,)), ((), ())), preferred_element_type=jnp.float32
    )


def column_sums(values):
    return jnp.sum(values.astype(jnp.float32), axis=0)


def lookup(lookup_table, wanted):
    entries = jnp.arange(lookup_table.shape[0], dtype=jnp.int32)
    matches = wanted[..., None] == entries
    located = jnp.sum(jnp.where(matches, lookup_table, jnp.int32(0)), axis=-1, dtype=jnp.int32)
    return jnp.where(wanted >= 0, located, jnp.int32(-1))


def ancestor_slots(block_segment, segment_parent, own_segments):
    entries = jnp.arange(block_segment.shape[0], dtype=jnp.int32)
    placed = block_segment[None, :] == entries[:, None]
    slot_of = jnp.sum(jnp.where(placed, entries[None, :], jnp.int32(0)), axis=1, dtype=jnp.int32)
    current = own_segments
    lineage = []
    for depth_step in range(DEPTH):
        lineage.append(current)
        current = lookup(segment_parent, current)
    lineage = jnp.stack(lineage, axis=-1)
    usable = lineage >= 0
    return (jnp.where(usable, lookup(slot_of, lineage), jnp.int32(0)), usable)


def key_mask(usable):
    query_row = jnp.arange(BLK, dtype=jnp.int32)[:, None]
    key_index = jnp.arange(DEPTH * BLK, dtype=jnp.int32)
    key_row = (key_index % BLK)[None, :]
    earlier = key_row <= query_row
    level_open = jnp.repeat(usable, BLK, axis=-1)
    own_level = (key_index < BLK)[None, :]
    return jnp.where(own_level, earlier, level_open[..., None, :])


def merge_heads(pieces):
    head_count, block_count, row_count, head_size = pieces.shape
    return jnp.transpose(pieces, (1, 2, 0, 3)).reshape(
        block_count, row_count, head_count * head_size
    )


def shards(
    inputs,
    cotangent,
    block_segment,
    segment_parent,
    query_weight,
    key_weight,
    value_weight,
    output_weight,
    gate_weight,
    gate_bias,
    up_weight,
    up_bias,
    down_weight,
    down_bias,
    carry_weight,
    carry_bias,
    first_gain,
    first_shift,
    second_gain,
    second_shift,
):
    forward_set = (
        lax.all_gather(query_weight, ("dp", "seq"), axis=0, tiled=True),
        lax.all_gather(key_weight, ("dp", "seq"), axis=0, tiled=True),
        lax.all_gather(value_weight, ("dp", "seq"), axis=0, tiled=True),
        lax.all_gather(output_weight, ("dp", "seq"), axis=0, tiled=True),
        lax.all_gather(gate_weight, ("dp", "seq"), axis=0, tiled=True),
        lax.all_gather(gate_bias, ("dp", "seq"), axis=0, tiled=True),
        lax.all_gather(up_weight, ("dp", "seq"), axis=0, tiled=True),
        lax.all_gather(up_bias, ("dp", "seq"), axis=0, tiled=True),
        lax.all_gather(down_weight, ("dp", "seq"), axis=0, tiled=True),
        lax.all_gather(down_bias, ("dp", "seq"), axis=0, tiled=True),
        lax.all_gather(carry_weight, ("dp", "seq"), axis=0, tiled=True),
        lax.all_gather(carry_bias, ("dp", "seq"), axis=0, tiled=True),
        lax.all_gather(first_gain, ("dp", "seq"), axis=0, tiled=True),
        lax.all_gather(first_shift, ("dp", "seq"), axis=0, tiled=True),
        lax.all_gather(second_gain, ("dp", "seq"), axis=0, tiled=True),
        lax.all_gather(second_shift, ("dp", "seq"), axis=0, tiled=True),
    )
    model_width = inputs.shape[1]
    head_count = model_width // HD
    score_scale = HD ** (-0.5)
    block_count = inputs.shape[0] // BLK
    group_blocks = block_segment.shape[0]
    own_start = lax.axis_index("seq") * block_count
    own_segments = lax.dynamic_slice_in_dim(block_segment, own_start, block_count)
    ancestor_slot, usable = ancestor_slots(block_segment, segment_parent, own_segments)
    allowed = key_mask(usable)
    values_in = inputs.astype(jnp.float32)
    first_scale = forward_set[12].astype(jnp.float32)
    first_offset = forward_set[13].astype(jnp.float32)
    normed = normalize(values_in, first_scale, first_offset)
    normed_low = normed.astype(jnp.bfloat16)
    query_low = matmul(normed_low, forward_set[0]).astype(jnp.bfloat16)
    gate_open = jax.nn.sigmoid(
        matmul(normed_low, forward_set[4]) + forward_set[5].astype(jnp.float32)
    )
    key_low = matmul(normed_low, forward_set[1]).astype(jnp.bfloat16)
    value_low = matmul(normed_low, forward_set[2]).astype(jnp.bfloat16)
    key_group, value_group = (
        lax.all_gather(key_low, "seq", axis=0, tiled=True),
        lax.all_gather(value_low, "seq", axis=0, tiled=True),
    )
    key_here = key_group.reshape(group_blocks, BLK, model_width)[ancestor_slot].reshape(
        block_count, DEPTH * BLK, model_width
    )
    value_here = value_group.reshape(group_blocks, BLK, model_width)[ancestor_slot].reshape(
        block_count, DEPTH * BLK, model_width
    )
    query_blocks = query_low.reshape(block_count, BLK, model_width)

    def head_forward(head_index):
        column_start = head_index * HD
        head_query_rows = lax.dynamic_slice_in_dim(query_blocks, column_start, HD, 2)
        head_key_rows = lax.dynamic_slice_in_dim(key_here, column_start, HD, 2)
        head_value_rows = lax.dynamic_slice_in_dim(value_here, column_start, HD, 2)
        scores = (
            jnp.einsum(
                "wgt,wyt->wgy", head_query_rows, head_key_rows, preferred_element_type=jnp.float32
            )
            * score_scale
        )
        scores = jnp.where(allowed, scores, NEGATIVE)
        highest = jnp.max(scores, axis=-1, keepdims=True)
        logsum = highest + jnp.log(jnp.sum(jnp.exp(scores - highest), axis=-1, keepdims=True))
        attention_weight = jnp.exp(scores - logsum).astype(jnp.bfloat16)
        return (
            jnp.einsum(
                "win,wnv->wiv",
                attention_weight,
                head_value_rows,
                preferred_element_type=jnp.float32,
            ),
            logsum,
        )

    head_mixed, log_normalizers = lax.map(head_forward, jnp.arange(head_count))
    attended_low = merge_heads(head_mixed).reshape(-1, model_width).astype(jnp.bfloat16)
    branch = matmul(attended_low, forward_set[3])
    middle = values_in + gate_open * branch
    second_scale = forward_set[14].astype(jnp.float32)
    second_offset = forward_set[15].astype(jnp.float32)
    normed_second = normalize(middle, second_scale, second_offset).astype(jnp.bfloat16)
    up_pre = matmul(normed_second, forward_set[6]) + forward_set[7].astype(jnp.float32)
    up_sigmoid = jax.nn.sigmoid(up_pre)
    hidden_low = (up_pre * up_sigmoid).astype(jnp.bfloat16)
    update = matmul(hidden_low, forward_set[8]) + forward_set[9].astype(jnp.float32)
    carry_open = jax.nn.sigmoid(
        matmul(normed_second, forward_set[10]) + forward_set[11].astype(jnp.float32)
    )
    output = (middle + carry_open * update).astype(jnp.bfloat16)
    backward_set = (
        lax.all_gather(query_weight, ("dp", "seq"), axis=0, tiled=True),
        lax.all_gather(key_weight, ("dp", "seq"), axis=0, tiled=True),
        lax.all_gather(value_weight, ("dp", "seq"), axis=0, tiled=True),
        lax.all_gather(output_weight, ("dp", "seq"), axis=0, tiled=True),
        lax.all_gather(gate_weight, ("dp", "seq"), axis=0, tiled=True),
        lax.all_gather(gate_bias, ("dp", "seq"), axis=0, tiled=True),
        lax.all_gather(up_weight, ("dp", "seq"), axis=0, tiled=True),
        lax.all_gather(up_bias, ("dp", "seq"), axis=0, tiled=True),
        lax.all_gather(down_weight, ("dp", "seq"), axis=0, tiled=True),
        lax.all_gather(down_bias, ("dp", "seq"), axis=0, tiled=True),
        lax.all_gather(carry_weight, ("dp", "seq"), axis=0, tiled=True),
        lax.all_gather(carry_bias, ("dp", "seq"), axis=0, tiled=True),
        lax.all_gather(first_gain, ("dp", "seq"), axis=0, tiled=True),
        lax.all_gather(first_shift, ("dp", "seq"), axis=0, tiled=True),
        lax.all_gather(second_gain, ("dp", "seq"), axis=0, tiled=True),
        lax.all_gather(second_shift, ("dp", "seq"), axis=0, tiled=True),
    )
    grad_out = cotangent.astype(jnp.float32)
    update_grad = (carry_open * grad_out).astype(jnp.bfloat16)
    carry_pre_grad = (grad_out * update * carry_open * (1.0 - carry_open)).astype(jnp.bfloat16)
    grad_down = inner_rows(hidden_low, update_grad)
    grad_down_bias = column_sums(update_grad)
    grad_carry = inner_rows(normed_second, carry_pre_grad)
    grad_carry_bias = column_sums(carry_pre_grad)
    silu_slope = up_sigmoid * (1.0 + up_pre * (1.0 - up_sigmoid))
    up_pre_grad = (against(update_grad, backward_set[8]) * silu_slope).astype(jnp.bfloat16)
    grad_up = inner_rows(normed_second, up_pre_grad)
    grad_up_bias = column_sums(up_pre_grad)
    second_norm_grad = against(up_pre_grad, backward_set[6]) + against(
        carry_pre_grad, backward_set[10]
    )
    second_pull = jax.vjp(
        normalize,
        middle,
        backward_set[14].astype(jnp.float32),
        backward_set[15].astype(jnp.float32),
    )[1]
    middle_part, grad_second_gain, grad_second_shift = second_pull(second_norm_grad)
    middle_grad = grad_out + middle_part
    branch_grad = (gate_open * middle_grad).astype(jnp.bfloat16)
    gate_pre_grad = (middle_grad * branch * gate_open * (1.0 - gate_open)).astype(jnp.bfloat16)
    grad_output = inner_rows(attended_low, branch_grad)
    grad_gate = inner_rows(normed_low, gate_pre_grad)
    grad_gate_bias = column_sums(gate_pre_grad)
    attended_grad = against(branch_grad, backward_set[3]).astype(jnp.bfloat16)
    attended_grad_blocks = attended_grad.reshape(block_count, BLK, model_width)

    def head_backward(packed):
        head_index, logsum = packed
        column_start = head_index * HD
        head_query_rows = lax.dynamic_slice_in_dim(query_blocks, column_start, HD, 2)
        head_key_rows = lax.dynamic_slice_in_dim(key_here, column_start, HD, 2)
        head_value_rows = lax.dynamic_slice_in_dim(value_here, column_start, HD, 2)
        head_gradient = lax.dynamic_slice_in_dim(attended_grad_blocks, column_start, HD, 2)
        scores = (
            jnp.einsum(
                "wgt,wyt->wgy", head_query_rows, head_key_rows, preferred_element_type=jnp.float32
            )
            * score_scale
        )
        scores = jnp.where(allowed, scores, NEGATIVE)
        shares = jnp.exp(scores - logsum)
        share_grad = jnp.einsum(
            "wgt,wyt->wgy", head_gradient, head_value_rows, preferred_element_type=jnp.float32
        )
        row_dot = jnp.sum(shares * share_grad, axis=-1, keepdims=True)
        score_gradient = (shares * (share_grad - row_dot)).astype(jnp.bfloat16)
        query_part = (
            jnp.einsum(
                "win,wnv->wiv", score_gradient, head_key_rows, preferred_element_type=jnp.float32
            )
            * score_scale
        )
        key_part = (
            jnp.einsum(
                "gow,gox->gwx", score_gradient, head_query_rows, preferred_element_type=jnp.float32
            )
            * score_scale
        )
        value_part = jnp.einsum(
            "gow,gox->gwx",
            shares.astype(jnp.bfloat16),
            head_gradient,
            preferred_element_type=jnp.float32,
        )
        return (query_part, key_part, value_part, row_dot)

    query_parts, key_parts, value_parts, row_dots = lax.map(
        head_backward, (jnp.arange(head_count), log_normalizers)
    )
    query_rows_grad = merge_heads(query_parts).reshape(-1, model_width).astype(jnp.bfloat16)
    flat_slots = ancestor_slot.reshape(-1)
    key_sums = (
        jnp.zeros((group_blocks, BLK, model_width), jnp.float32)
        .at[flat_slots]
        .add(merge_heads(key_parts).reshape(-1, BLK, model_width))
    )
    value_sums = (
        jnp.zeros((group_blocks, BLK, model_width), jnp.float32)
        .at[flat_slots]
        .add(merge_heads(value_parts).reshape(-1, BLK, model_width))
    )
    key_total, value_total = (
        lax.psum_scatter(
            key_sums.reshape(-1, model_width).astype(jnp.bfloat16),
            "seq",
            scatter_dimension=0,
            tiled=True,
        ).astype(jnp.float32),
        lax.psum_scatter(
            value_sums.reshape(-1, model_width).astype(jnp.bfloat16),
            "seq",
            scatter_dimension=0,
            tiled=True,
        ).astype(jnp.float32),
    )
    key_rows_grad = key_total.astype(jnp.bfloat16)
    value_rows_grad = value_total.astype(jnp.bfloat16)
    grad_query = inner_rows(normed_low, query_rows_grad)
    grad_key = inner_rows(normed_low, key_rows_grad)
    grad_value = inner_rows(normed_low, value_rows_grad)
    first_norm_grad = (
        against(query_rows_grad, backward_set[0])
        + against(key_rows_grad, backward_set[1])
        + against(value_rows_grad, backward_set[2])
        + against(gate_pre_grad, backward_set[4])
    )
    first_pull = jax.vjp(
        normalize,
        values_in,
        backward_set[12].astype(jnp.float32),
        backward_set[13].astype(jnp.float32),
    )[1]
    input_part, grad_first_gain, grad_first_shift = first_pull(first_norm_grad)
    input_grad = middle_grad + input_part
    owned = (
        lax.psum_scatter(grad_query, ("dp", "seq"), scatter_dimension=0, tiled=True),
        lax.psum_scatter(grad_key, ("dp", "seq"), scatter_dimension=0, tiled=True),
        lax.psum_scatter(grad_value, ("dp", "seq"), scatter_dimension=0, tiled=True),
        lax.psum_scatter(grad_output, ("dp", "seq"), scatter_dimension=0, tiled=True),
        lax.psum_scatter(grad_gate, ("dp", "seq"), scatter_dimension=0, tiled=True),
        lax.psum_scatter(grad_gate_bias, ("dp", "seq"), scatter_dimension=0, tiled=True),
        lax.psum_scatter(grad_up, ("dp", "seq"), scatter_dimension=0, tiled=True),
        lax.psum_scatter(grad_up_bias, ("dp", "seq"), scatter_dimension=0, tiled=True),
        lax.psum_scatter(grad_down, ("dp", "seq"), scatter_dimension=0, tiled=True),
        lax.psum_scatter(grad_down_bias, ("dp", "seq"), scatter_dimension=0, tiled=True),
        lax.psum_scatter(grad_carry, ("dp", "seq"), scatter_dimension=0, tiled=True),
        lax.psum_scatter(grad_carry_bias, ("dp", "seq"), scatter_dimension=0, tiled=True),
        lax.psum_scatter(grad_first_gain, ("dp", "seq"), scatter_dimension=0, tiled=True),
        lax.psum_scatter(grad_first_shift, ("dp", "seq"), scatter_dimension=0, tiled=True),
        lax.psum_scatter(grad_second_gain, ("dp", "seq"), scatter_dimension=0, tiled=True),
        lax.psum_scatter(grad_second_shift, ("dp", "seq"), scatter_dimension=0, tiled=True),
    )
    return (output, input_grad) + tuple(owned)


def solution(mesh):
    return jax.shard_map(
        shards,
        mesh=mesh,
        in_specs=(
            P(("dp", "seq"), None),
            P(("dp", "seq"), None),
            P("dp"),
            P("dp"),
            P(("dp", "seq"), None),
            P(("dp", "seq"), None),
            P(("dp", "seq"), None),
            P(("dp", "seq"), None),
            P(("dp", "seq"), None),
            P(("dp", "seq")),
            P(("dp", "seq"), None),
            P(("dp", "seq")),
            P(("dp", "seq"), None),
            P(("dp", "seq")),
            P(("dp", "seq"), None),
            P(("dp", "seq")),
            P(("dp", "seq")),
            P(("dp", "seq")),
            P(("dp", "seq")),
            P(("dp", "seq")),
        ),
        out_specs=(
            P(("dp", "seq"), None),
            P(("dp", "seq"), None),
            P(("dp", "seq"), None),
            P(("dp", "seq"), None),
            P(("dp", "seq"), None),
            P(("dp", "seq"), None),
            P(("dp", "seq"), None),
            P(("dp", "seq")),
            P(("dp", "seq"), None),
            P(("dp", "seq")),
            P(("dp", "seq"), None),
            P(("dp", "seq")),
            P(("dp", "seq"), None),
            P(("dp", "seq")),
            P(("dp", "seq")),
            P(("dp", "seq")),
            P(("dp", "seq")),
            P(("dp", "seq")),
        ),
        check_vma=False,
    )
```

profile of v0, /device:TPU:28, one launch (start us, length us, event | category | flops | bytes accessed | tf_op | source)
XLA Modules:
  0.0 2102.8 jit_solution(12160083234098167587)
XLA Ops:
  14.0 40.1 %all-reduce.17 = (bf16[512]{0:T(512)(128)(2,1)S(1)}, bf16[512]{0:T(512)(128)(2,1)S(1)}, bf16[512]{0:T(512)(128)(2,1)S(1)}, bf16[512]{0:T(512)(128)(2,1)S(1)}, bf...) all-reduce(bf16[512]{0:T(512)(128)(2,1)S(1)} %dynamic-update-slice., ...), channel_id=1, replica_groups=mesh['dp'=4,'seq'=8] {'dp','seq'}, use_global_device_ids=true, to_apply=%add.2 | all-reduce | flops 5632 | bytes 22528
  56.0 60.1 %all_gather.71 = bf16[512,512]{1,0:T(8,128)(2,1)S(1)} all-gather(bf16[16,512]{1,0:T(8,128)(2,1)S(1)} %copy-done.37), channel_id=1, replica_groups=mesh['dp'=4,'seq'=8] {'dp','seq'}, dimensions={0}, use_global_device_ids=true | all-gather | bytes 540672 | tf_op jit(solution)/shard_map/all_gather | solution.py:104
  118.6 73.0 %all_gather.69 = bf16[512,512]{1,0:T(8,128)(2,1)S(1)} all-gather(bf16[16,512]{1,0:T(8,128)(2,1)S(1)} %copy-done.38), channel_id=1, replica_groups=mesh['dp'=4,'seq'=8] {'dp','seq'}, dimensions={0}, use_global_device_ids=true | all-gather | bytes 540672 | tf_op jit(solution)/shard_map/all_gather | solution.py:103
  199.2 70.5 %all_gather.68 = bf16[512,512]{1,0:T(8,128)(2,1)S(1)} all-gather(bf16[16,512]{1,0:T(8,128)(2,1)S(1)} %copy-done.39), channel_id=1, replica_groups=mesh['dp'=4,'seq'=8] {'dp','seq'}, dimensions={0}, use_global_device_ids=true | all-gather | bytes 540672 | tf_op jit(solution)/shard_map/all_gather | solution.py:102
  271.2 74.0 %all_gather.73 = bf16[512,512]{1,0:T(8,128)(2,1)} all-gather(bf16[16,512]{1,0:T(8,128)(2,1)S(1)} %copy-done.40), channel_id=1, replica_groups=mesh['dp'=4,'seq'=8] {'dp','seq'}, dimensions={0}, use_global_device_ids=true | all-gather | bytes 540672 | tf_op jit(solution)/shard_map/all_gather | solution.py:105
  345.2 72.4 %all_gather.66 = bf16[512,512]{1,0:T(8,128)(2,1)} all-gather(bf16[16,512]{1,0:T(8,128)(2,1)S(1)} %copy-done.41), channel_id=1, replica_groups=mesh['dp'=4,'seq'=8] {'dp','seq'}, dimensions={0}, use_global_device_ids=true | all-gather | bytes 540672 | tf_op jit(solution)/shard_map/all_gather | solution.py:106
  418.0 73.1 %all_gather.76 = bf16[512,512]{1,0:T(8,128)(2,1)} all-gather(bf16[16,512]{1,0:T(8,128)(2,1)S(1)} %copy-done.42), channel_id=1, replica_groups=mesh['dp'=4,'seq'=8] {'dp','seq'}, dimensions={0}, use_global_device_ids=true | all-gather | bytes 540672 | tf_op jit(solution)/shard_map/all_gather | solution.py:112
  491.1 7.5 gather_fusion.1
  498.6 9.5 copy.191
  508.1 7.5 gather_fusion
  515.6 9.5 copy.190
  525.3 48.4 %while.28 = (s32[]{:T(128)}, bf16[8,5,128,64]{2,3,1,0:T(8,128)(2,1)S(1)}, f32[8,5,128,1]{2,1,3,0:T(8,128)S(1)}, s32[8]{0:T(128)S(1)}, bf16[5,128,512]{1,2,0:T(8,...) while((s32[]{:T(128)}, ...), condition=%wide.region_16.17_spmd.clone, body=%wide.region_13.16_spmd.clone.sunk | while | flops 216268160 | bytes 11920583 | solution.py:176
  579.0 7.2 multiply_convert_fusion.2
  586.1 4.3 convolution_add_fusion.5
  590.5 2.8 convert_reduce_fusion.2
  593.8 3.6 convert_reduce_fusion
  607.9 100.5 %while.29 = (s32[]{:T(128)}, bf16[8,5,128,64]{2,3,1,0:T(8,128)(2,1)}, f32[8,5,1280,64]{2,3,1,0:T(8,128)}, f32[8,5,1280,64]{2,3,1,0:T(8,128)}, s32[8]{0:T(128)S(1...) while((s32[]{:T(128)}, ...), condition=%wide.region_23.24_spmd.clone, body=%wide.region_21.23_spmd.clone.sunk | while | flops 532929920 | bytes 30990056 | solution.py:279
  611.0 2.7 multiply_reduce_fusion.5
  661.3 2.7 multiply_reduce_fusion.5
  686.3 2.7 multiply_reduce_fusion.5
  708.4 19.3 copy.221
  727.7 22.3 %reshape.437 = f32[50,128,512]{2,1,0:T(8,128)} reshape(f32[5,1280,8,64]{3,2,1,0:T(8,128)} %copy.221) | data formatting | bytes 26214400 | tf_op jit(solution)/shard_map/reshape;reshape | solution.py:287
  750.0 5.3 broadcast.248.clone.1
  755.3 31.7 %scatter_fusion = f32[40,128,512]{2,1,0:T(8,128)} fusion(f32[40,128,512]{2,1,0:T(8,128)} %broadcast.248.clone.1, s32[50]{0:T(128)S(1)} %fusion.77, f32[50,128,512]{2,1,0:T(8,128)} %reshape.437), kind=kCustom, calls=%fused_computation.2 | custom fusion | flops 3276800 | bytes 39321800 | tf_op jit(solution)/shard_map/scatter-add | solution.py:287
  787.0 7.1 convert_element_type.154
  794.1 19.9 copy.222
  814.0 22.5 %reshape.438 = f32[50,128,512]{2,1,0:T(8,128)} reshape(f32[5,1280,8,64]{3,2,1,0:T(8,128)} %copy.222) | data formatting | bytes 26214400 | tf_op jit(solution)/shard_map/reshape;reshape | solution.py:292
  836.5 5.3 broadcast.248.clone
  841.8 31.9 %scatter_fusion.1 = f32[40,128,512]{2,1,0:T(8,128)} fusion(f32[40,128,512]{2,1,0:T(8,128)} %broadcast.248.clone, s32[50]{0:T(128)S(1)} %fusion.77, f32[50,128,512]{2,1,0:T(8,128)} %reshape.438), kind=kCustom, calls=%fused_computation.3 | custom fusion | flops 3276800 | bytes 39321800 | tf_op jit(solution)/shard_map/scatter-add | solution.py:292
  873.8 7.1 convert_element_type.156
  884.7 2.8 fusion.63
  892.0 2.7 fusion.79
  894.8 5.6 fusion.97
  901.5 5.6 fusion.101
  907.2 2.7 fusion.83
  912.0 95.9 %reduce-scatter.13.cloned.1.call-done = bf16[640,512]{1,0:T(8,128)(2,1)} async-done(((bf16[5120,512]{1,0:T(8,128)(2,1)}), bf16[640,512]{1,0:T(8,128)(2,1)}) %reduce-scatter.13.cloned.1.call-update) | async-done | bytes 655376 | tf_op jit(solution)/shard_map/reduce_scatter | solution.py:301
  1007.9 2.7 fusion.81
  1016.6 41.4 %all-reduce.16 = (f32[512]{0:T(512)S(1)}, f32[2048]{0:T(1024)S(1)}, f32[512]{0:T(512)S(1)}, f32[512]{0:T(512)S(1)}, f32[512]{0:T(512)S(1)}, /*index=5*/f32[512]{0:T(512)S(1)}, f32[512]{0:T(512)S(1)}, f32[512]{0:T(512)S(1)}) all-reduce(f32[512]{0:T(512)S(1)} %get-tuple-element.502, ...), channel_id=9, replica_groups=mesh['dp'=4,'seq'=8] {'dp','seq'}, use_global_device_ids=true, to_apply=%region_36.37.clone | all-reduce | flops 5632 | bytes 45056
  1062.2 2.8 add_add_fusion.2
  1065.0 2.8 copy.212
  1068.3 69.3 %reduce-scatter.29.cloned.1.call-done = f32[16,512]{1,0:T(8,128)} async-done(((f32[512,512]{1,0:T(8,128)}), f32[16,512]{1,0:T(8,128)}) %reduce-scatter.29.cloned.1.call-update) | async-done | bytes 32784 | tf_op jit(solution)/shard_map/reduce_scatter | solution.py:338
  1137.7 134.2 %reduce-scatter.21.cloned.1.call-done = f32[16,512]{1,0:T(8,128)} async-done(((f32[512,512]{1,0:T(8,128)}), f32[16,512]{1,0:T(8,128)}) %reduce-scatter.21.cloned.1.call-update) | async-done | bytes 32784 | tf_op jit(solution)/shard_map/reduce_scatter | solution.py:331
  1271.9 134.2 %reduce-scatter.15.cloned.1.call-done = f32[16,512]{1,0:T(8,128)} async-done(((f32[512,512]{1,0:T(8,128)}), f32[16,512]{1,0:T(8,128)}) %reduce-scatter.15.cloned.1.call-update) | async-done | bytes 32784 | tf_op jit(solution)/shard_map/reduce_scatter | solution.py:328
  1406.0 134.1 %reduce-scatter.23.cloned.1.call-done = f32[16,512]{1,0:T(8,128)} async-done(((f32[512,512]{1,0:T(8,128)}), f32[16,512]{1,0:T(8,128)}) %reduce-scatter.23.cloned.1.call-update) | async-done | bytes 32784 | tf_op jit(solution)/shard_map/reduce_scatter | solution.py:332
  1540.1 143.9 %reduce-scatter.25.cloned.1.call-done = f32[16,2048]{1,0:T(8,128)} async-done(((f32[512,2048]{1,0:T(8,128)}), f32[16,2048]{1,0:T(8,128)}) %reduce-scatter.25.cloned.1.call-update) | async-done | bytes 131088 | tf_op jit(solution)/shard_map/reduce_scatter | solution.py:334
  1684.0 142.1 %reduce-scatter.27.cloned.1.call-done = f32[64,512]{1,0:T(8,128)} async-done(((f32[2048,512]{1,0:T(8,128)}), f32[64,512]{1,0:T(8,128)}) %reduce-scatter.27.cloned.1.call-update) | async-done | bytes 131088 | tf_op jit(solution)/shard_map/reduce_scatter | solution.py:336
  1826.1 135.7 %reduce-scatter.17.cloned.1.call-done = f32[16,512]{1,0:T(8,128)} async-done(((f32[512,512]{1,0:T(8,128)}), f32[16,512]{1,0:T(8,128)}) %reduce-scatter.17.cloned.1.call-update) | async-done | bytes 32784 | tf_op jit(solution)/shard_map/reduce_scatter | solution.py:329
  1961.9 134.1 %reduce-scatter.19.cloned.1.call-done = f32[16,512]{1,0:T(8,128)} async-done(((f32[512,512]{1,0:T(8,128)}), f32[16,512]{1,0:T(8,128)}) %reduce-scatter.19.cloned.1.call-update) | async-done | bytes 32784 | tf_op jit(solution)/shard_map/reduce_scatter | solution.py:330
  (371 shorter events, 188.5 us)
Async XLA Ops:
  7.2 483.9 %all-gather.7.cloned.1.call-start = ((), (), s32[]{:S(2)}) async-start(), calls=%async_computation.11 | async-start | bytes 5898240 | tf_op jit(solution)/shard_map/all_gather | solution.py:141
  54.2 522.5 %copy-start.35 = (f32[512]{0:T(512)}, f32[512]{0:T(512)S(1)}, u32[]{:S(2)}) copy-start(f32[512]{0:T(512)S(1)} %convert_element_type.127) | copy-start | bytes 6148
  54.2 522.5 %copy-start.46 = (f32[512]{0:T(512)}, f32[512]{0:T(512)S(1)}, u32[]{:S(2)}) copy-start(f32[512]{0:T(512)S(1)} %convert_element_type.128) | copy-start | bytes 6148
  54.2 1.8 copy-start.37
  55.6 521.1 %copy-start = (bf16[640,512]{0,1:T(8,128)(2,1)}, bf16[640,512]{0,1:T(8,128)(2,1)S(1)}, u32[]{:S(2)}) copy-start(bf16[640,512]{0,1:T(8,128)(2,1)S(1)} %copy.176) | copy-start | bytes 1966084
  55.8 520.9 %copy-start.29 = (f32[640]{0:T(1024)}, f32[640]{0:T(1024)S(1)}, u32[]{:S(2)}) copy-start(f32[640]{0:T(1024)S(1)} %broadcast_multiply_fusion.1) | copy-start | bytes 7684
  56.0 62.5 %copy-start.31 = (f32[640]{0:T(1024)}, f32[640]{0:T(1024)S(1)}, u32[]{:S(2)}) copy-start(f32[640]{0:T(1024)S(1)} %fusion.54) | copy-start | bytes 7684
  56.0 520.7 %copy-start.33 = (f32[640]{0:T(1024)}, f32[640]{0:T(1024)S(1)}, u32[]{:S(2)}) copy-start(f32[640]{0:T(1024)S(1)} %fusion.75) | copy-start | bytes 7684
  117.0 1.6 copy-start.38
  118.5 389.6 %all-gather.5.cloned.1.call-start = ((), (), s32[]{:S(2)}) async-start(), calls=%async_computation.10 | async-start | bytes 5898240 | tf_op jit(solution)/shard_map/all_gather | solution.py:140
  192.4 3.0 copy-start.50
  192.4 3.2 copy-start.53
  192.4 6.8 copy-start.39
  194.0 385.0 %all-gather.9.cloned.1.call-start = ((), (), s32[]{:S(2)}) async-start(), calls=%async_computation.12 | async-start | bytes 2162688 | tf_op jit(solution)/shard_map/all_gather | solution.py:108
  194.7 391.4 %all-gather.11.cloned.1.call-start = ((), (), s32[]{:S(2)}) async-start(), calls=%async_computation.13 | async-start | bytes 2162688 | tf_op jit(solution)/shard_map/all_gather | solution.py:110
  195.3 711.8 %reduce-scatter.11.cloned.1.call-start = ((), (), s32[]{:S(2)}) async-start(), calls=%async_computation.14 | async-start | bytes 5898240 | tf_op jit(solution)/shard_map/reduce_scatter | solution.py:295
  270.5 74.7 %copy-start.41 = (bf16[16,512]{1,0:T(8,128)(2,1)S(1)}, bf16[16,512]{1,0:T(8,128)(2,1)}, u32[]{:S(2)}) copy-start(bf16[16,512]{1,0:T(8,128)(2,1)} %param.32) | copy-start | bytes 49156
  270.5 147.2 %copy-start.26 = (bf16[640,512]{1,0:T(8,128)(2,1)S(1)}, bf16[640,512]{1,0:T(8,128)(2,1)}, u32[]{:S(2)}) copy-start(bf16[640,512]{1,0:T(8,128)(2,1)} %param.25) | copy-start | bytes 1966084
  270.8 147.2 %copy-start.42 = (bf16[16,512]{1,0:T(8,128)(2,1)S(1)}, bf16[16,512]{1,0:T(8,128)(2,1)}, u32[]{:S(2)}) copy-start(bf16[16,512]{1,0:T(8,128)(2,1)} %param.38) | copy-start | bytes 49156
  418.0 172.4 %copy-start.2 = (bf16[640,512]{0,1:T(8,128)(2,1)}, bf16[640,512]{0,1:T(8,128)(2,1)S(1)}, u32[]{:S(2)}) copy-start(bf16[640,512]{0,1:T(8,128)(2,1)S(1)} %copy.195) | copy-start | bytes 1966084
  573.7 2.3 copy-start.19
  575.1 1.7 copy-start.17
  576.7 2.0 copy-start.5
  586.1 4.3 copy-start.21
  590.5 2.8 copy-start.52
  590.5 3.4 copy-start.57
  593.3 4.2 copy-start.55
  593.3 6.0 copy-start.24
  593.8 3.6 copy-start.51
  597.4 1.8 copy-start.54
  600.8 1.5 copy-start.6
  600.8 1.9 copy-start.23
  794.1 213.9 %reduce-scatter.13.cloned.1.call-start = ((), (), s32[]{:S(2)}) async-start(), calls=%async_computation.15 | async-start | bytes 5898240 | tf_op jit(solution)/shard_map/reduce_scatter | solution.py:301
  880.9 256.7 %reduce-scatter.29.cloned.1.call-start = ((), (), s32[]{:S(2)}) async-start(), calls=%async_computation.23 | async-start | bytes 1081344 | tf_op jit(solution)/shard_map/reduce_scatter | solution.py:338
  883.6 388.2 %reduce-scatter.21.cloned.1.call-start = ((), (), s32[]{:S(2)}) async-start(), calls=%async_computation.19 | async-start | bytes 1081344 | tf_op jit(solution)/shard_map/reduce_scatter | solution.py:331
  887.5 2.7 copy-start.1
  887.5 2.7 copy-start.30
  887.5 2.7 copy-start.34
  887.5 2.7 copy-start.36
  887.5 2.7 copy-start.47
  887.6 518.4 %reduce-scatter.15.cloned.1.call-start = ((), (), s32[]{:S(2)}) async-start(), calls=%async_computation.16 | async-start | bytes 1081344 | tf_op jit(solution)/shard_map/reduce_scatter | solution.py:328
  892.0 648.2 %reduce-scatter.23.cloned.1.call-start = ((), (), s32[]{:S(2)}) async-start(), calls=%async_computation.20 | async-start | bytes 1081344 | tf_op jit(solution)/shard_map/reduce_scatter | solution.py:332
  894.7 789.3 %reduce-scatter.25.cloned.1.call-start = ((), (), s32[]{:S(2)}) async-start(), calls=%async_computation.21 | async-start | bytes 4325376 | tf_op jit(solution)/shard_map/reduce_scatter | solution.py:334
  900.4 925.7 %reduce-scatter.27.cloned.1.call-start = ((), (), s32[]{:S(2)}) async-start(), calls=%async_computation.22 | async-start | bytes 4325376 | tf_op jit(solution)/shard_map/reduce_scatter | solution.py:336
  907.1 1054.8 %reduce-scatter.17.cloned.1.call-start = ((), (), s32[]{:S(2)}) async-start(), calls=%async_computation.17 | async-start | bytes 1081344 | tf_op jit(solution)/shard_map/reduce_scatter | solution.py:329
  909.9 1186.1 %reduce-scatter.19.cloned.1.call-start = ((), (), s32[]{:S(2)}) async-start(), calls=%async_computation.18 | async-start | bytes 1081344 | tf_op jit(solution)/shard_map/reduce_scatter | solution.py:330
  1010.7 2.0 copy-start.13
  1010.7 2.0 copy-start.28
  (24 other events, 23.2 us)
Sparse Core Ops, SparseCore 0:
  118.7 97.2 all-gather.6
  218.7 91.7 all-gather.4
  313.6 56.3 all-gather.8
  372.8 55.8 all-gather.10
  794.2 107.9 reduce-scatter.10
  905.6 102.3 reduce-scatter.12
  1010.8 126.8 reduce-scatter.28
  1140.6 131.2 reduce-scatter.20
  1274.7 131.2 reduce-scatter.14
  1408.8 131.2 reduce-scatter.22
  1543.0 141.0 reduce-scatter.24
  1686.8 139.3 reduce-scatter.26
  1828.9 132.8 reduce-scatter.16
  1964.6 131.3 reduce-scatter.18
where the time goes:
time: 2130 us; the launch traced here: 2100 us
  waiting for transfers between devices  1130 us (53%)
  blocking collectives  505 us (24%)
  matrix products  179 us (8%)
  local copies, waits for them, and re-layouts  174 us (8%)
  other arithmetic  93.8 us (4%)
    reduce_scatter x1, waiting for transfers between devices, shards(): lax.psum_scatter(grad_up, ('dp', 'seq'), scatter_dimension=0, tiled=True)  144 us
    reduce_scatter x1, waiting for transfers between devices, shards(): lax.psum_scatter(grad_down, ('dp', 'seq'), scatter_dimension=0, tiled=True)  142 us
    reduce_scatter x1, waiting for transfers between devices, shards(): lax.psum_scatter(grad_key, ('dp', 'seq'), scatter_dimension=0, tiled=True)  136 us
    reduce_scatter x1, waiting for transfers between devices, shards(): lax.psum_scatter(grad_output, ('dp', 'seq'), scatter_dimension=0, tiled=T...  134 us
    reduce_scatter x1, waiting for transfers between devices, shards(): lax.psum_scatter(grad_query, ('dp', 'seq'), scatter_dimension=0, tiled=True)  134 us
    reduce_scatter x1, waiting for transfers between devices, shards(): lax.psum_scatter(grad_value, ('dp', 'seq'), scatter_dimension=0, tiled=True)  134 us
    reduce_scatter x1, waiting for transfers between devices, shards(): lax.psum_scatter(grad_gate, ('dp', 'seq'), scatter_dimension=0, tiled=True)  134 us
    reduce_scatter x1, waiting for transfers between devices, shards(): lax.psum_scatter(value_sums.reshape(-1, model_width).astype(jnp.bfloat16)...  95.9 us
  transfers between devices with their start and end apart: 14, of which 9 were waited for; matrix products, arithmetic and copies ran while one was open for 11% of the time, Pallas kernels for 0%

commit v1 on v0

v1 whole, which is shorter than its diff:
```python
import functools

import jax
import jax.numpy as jnp
from jax import lax
from jax.experimental import pallas as pl
from jax.experimental.pallas import tpu as pltpu
from jax.sharding import PartitionSpec as P

HD = 64
BLK = 128
DEPTH = 10
PAIR = 2 * HD

EPSILON = 1e-05
NEGATIVE = -1e30
BOTH = ("dp", "seq")
VMEM_BYTES = 60 * 1024 * 1024


def normalize(values, norm_gain, norm_shift):
    center = values - jnp.mean(values, axis=-1, keepdims=True)
    spread = jnp.mean(center * center, axis=-1, keepdims=True)
    return center * lax.rsqrt(spread + EPSILON) * norm_gain + norm_shift


def matmul(left_side, right_side):
    return jnp.dot(left_side, right_side, preferred_element_type=jnp.float32)


def inner_rows(left_side, right_side):
    return lax.dot_general(
        left_side, right_side, (((0,), (0,)), ((), ())), preferred_element_type=jnp.float32
    )


def against(left_side, right_side):
    return lax.dot_general(
        left_side, right_side, (((1,), (1,)), ((), ())), preferred_element_type=jnp.float32
    )


def column_sums(values):
    return jnp.sum(values.astype(jnp.float32), axis=0)


def lookup(lookup_table, wanted):
    entries = jnp.arange(lookup_table.shape[0], dtype=jnp.int32)
    matches = wanted[..., None] == entries
    located = jnp.sum(jnp.where(matches, lookup_table, jnp.int32(0)), axis=-1, dtype=jnp.int32)
    return jnp.where(wanted >= 0, located, jnp.int32(-1))


def ancestor_slots(block_segment, segment_parent, own_segments):
    entries = jnp.arange(block_segment.shape[0], dtype=jnp.int32)
    placed = block_segment[None, :] == entries[:, None]
    slot_of = jnp.sum(jnp.where(placed, entries[None, :], jnp.int32(0)), axis=1, dtype=jnp.int32)
    current = own_segments
    lineage = []
    for depth_step in range(DEPTH):
        lineage.append(current)
        current = lookup(segment_parent, current)
    lineage = jnp.stack(lineage, axis=-1)
    usable = lineage >= 0
    return (jnp.where(usable, lookup(slot_of, lineage), jnp.int32(0)), usable)


def stack_heads(rows):
    lane = lax.broadcasted_iota(jnp.int32, rows.shape, 1)
    low = lane < HD
    zero = jnp.zeros_like(rows)
    return jnp.concatenate([jnp.where(low, rows, zero), jnp.where(low, zero, rows)], axis=0)


def unstack_heads(rows):
    half = rows.shape[0] // 2
    lane = lax.broadcasted_iota(jnp.int32, (half, rows.shape[1]), 1)
    return jnp.where(lane < HD, rows[:half], rows[half:])


def make_bias(levels, bias_ref):
    row = lax.broadcasted_iota(jnp.int32, (BLK, DEPTH * BLK), 0)
    col = lax.broadcasted_iota(jnp.int32, (BLK, DEPTH * BLK), 1)
    limit = jnp.where(col < BLK, row + 1, levels * BLK)
    bias = jnp.where(col < limit, jnp.float32(0.0), jnp.float32(NEGATIVE))
    bias_ref[:BLK, :] = bias
    bias_ref[BLK:, :] = bias


def fetch_levels(slots_ref, slot, source_ref, target_ref):
    for level in range(DEPTH):
        start = pl.multiple_of(slots_ref[slot, level] * BLK, BLK)
        target_ref[level * BLK : (level + 1) * BLK, :] = source_ref[pl.ds(start, BLK), :]


def forward_kernel(slots_ref, query_ref, key_ref, value_ref, mixed_ref, logsum_ref, key_here, value_here, bias_ref):
    width = query_ref.shape[1]

    def one_slot(slot, carry):
        rows = pl.ds(pl.multiple_of(slot * BLK, BLK), BLK)
        fetch_levels(slots_ref, slot, key_ref, key_here)
        fetch_levels(slots_ref, slot, value_ref, value_here)
        make_bias(slots_ref[slot, DEPTH], bias_ref)
        lane = lax.broadcasted_iota(jnp.int32, (BLK, PAIR), 1)
        logsums = jnp.zeros((BLK, PAIR), jnp.float32)
        for pair in range(width // PAIR):
            cols = slice(pair * PAIR, (pair + 1) * PAIR)
            stacked = stack_heads(query_ref[rows, cols])
            scores = against(stacked, key_here[:, cols]) + bias_ref[...]
            highest = jnp.max(scores, axis=-1, keepdims=True)
            raised = jnp.exp(scores - highest)
            total = jnp.sum(raised, axis=-1, keepdims=True)
            mixed = matmul(raised.astype(jnp.bfloat16), value_here[:, cols]) / total
            mixed_ref[rows, cols] = unstack_heads(mixed).astype(jnp.bfloat16)
            logsum = highest + jnp.log(total)
            logsums = jnp.where(lane == 2 * pair, logsum[:BLK], logsums)
            logsums = jnp.where(lane == 2 * pair + 1, logsum[BLK:], logsums)
        logsum_ref[rows, :] = logsums
        return carry

    lax.fori_loop(0, query_ref.shape[0] // BLK, one_slot, 0)


def backward_kernel(
    slots_ref,
    query_ref,
    key_ref,
    value_ref,
    logsum_ref,
    mixed_ref,
    mixed_grad_ref,
    query_grad_ref,
    sums_ref,
    key_here,
    value_here,
    bias_ref,
    key_sums,
    value_sums,
):
    width = query_ref.shape[1]
    key_sums[...] = jnp.zeros_like(key_sums)
    value_sums[...] = jnp.zeros_like(value_sums)

    def one_slot(slot, carry):
        rows = pl.ds(pl.multiple_of(slot * BLK, BLK), BLK)
        fetch_levels(slots_ref, slot, key_ref, key_here)
        fetch_levels(slots_ref, slot, value_ref, value_here)
        make_bias(slots_ref[slot, DEPTH], bias_ref)
        for pair in range(width // PAIR):
            cols = slice(pair * PAIR, (pair + 1) * PAIR)
            stacked = stack_heads(query_ref[rows, cols])
            grad_rows = mixed_grad_ref[rows, cols]
            grad_stacked = stack_heads(grad_rows)
            products = grad_rows.astype(jnp.float32) * mixed_ref[rows, cols].astype(jnp.float32)
            row_dot = jnp.sum(stack_heads(products), axis=-1, keepdims=True)
            logsum = jnp.concatenate(
                [logsum_ref[rows, 2 * pair : 2 * pair + 1], logsum_ref[rows, 2 * pair + 1 : 2 * pair + 2]], axis=0
            )
            key_rows = key_here[:, cols]
            shares = jnp.exp(against(stacked, key_rows) + bias_ref[...] - logsum)
            share_grad = against(grad_stacked, value_here[:, cols])
            score_grad = (shares * (share_grad - row_dot)).astype(jnp.bfloat16)
            query_grad = unstack_heads(matmul(score_grad, key_rows)) * (HD ** (-0.5))
            query_grad_ref[rows, cols] = query_grad.astype(jnp.bfloat16)
            key_part = inner_rows(stacked, score_grad)
            value_part = inner_rows(grad_stacked, shares.astype(jnp.bfloat16))
            for level in range(DEPTH):
                start = pl.multiple_of(slots_ref[slot, level] * BLK, BLK)
                here = slice(level * BLK, (level + 1) * BLK)
                key_sums[cols, pl.ds(start, BLK)] += key_part[:, here]
                value_sums[cols, pl.ds(start, BLK)] += value_part[:, here]
        return carry

    lax.fori_loop(0, query_ref.shape[0] // BLK, one_slot, 0)
    sums_ref[:width, :] = key_sums[...].astype(jnp.bfloat16)
    sums_ref[width:, :] = value_sums[...].astype(jnp.bfloat16)


def in_vmem():
    return pl.BlockSpec(memory_space=pltpu.VMEM)


def in_smem():
    return pl.BlockSpec(memory_space=pltpu.SMEM)


def attend(slots, query_rows, key_group, value_group):
    rows, width = query_rows.shape
    return pl.pallas_call(
        forward_kernel,
        out_shape=(
            jax.ShapeDtypeStruct((rows, width), jnp.bfloat16),
            jax.ShapeDtypeStruct((rows, PAIR), jnp.float32),
        ),
        in_specs=[in_smem(), in_vmem(), in_vmem(), in_vmem()],
        out_specs=(in_vmem(), in_vmem()),
        scratch_shapes=[
            pltpu.VMEM((DEPTH * BLK, width), jnp.bfloat16),
            pltpu.VMEM((DEPTH * BLK, width), jnp.bfloat16),
            pltpu.VMEM((2 * BLK, DEPTH * BLK), jnp.float32),
        ],
        compiler_params=pltpu.CompilerParams(vmem_limit_bytes=VMEM_BYTES),
    )(slots, query_rows, key_group, value_group)


def attend_backward(slots, query_rows, key_group, value_group, logsum, mixed, mixed_grad):
    rows, width = query_rows.shape
    keys = key_group.shape[0]
    return pl.pallas_call(
        backward_kernel,
        out_shape=(
            jax.ShapeDtypeStruct((rows, width), jnp.bfloat16),
            jax.ShapeDtypeStruct((2 * width, keys), jnp.bfloat16),
        ),
        in_specs=[in_smem()] + [in_vmem()] * 6,
        out_specs=(in_vmem(), in_vmem()),
        scratch_shapes=[
            pltpu.VMEM((DEPTH * BLK, width), jnp.bfloat16),
            pltpu.VMEM((DEPTH * BLK, width), jnp.bfloat16),
            pltpu.VMEM((2 * BLK, DEPTH * BLK), jnp.float32),
            pltpu.VMEM((width, keys), jnp.float32),
            pltpu.VMEM((width, keys), jnp.float32),
        ],
        compiler_params=pltpu.CompilerParams(vmem_limit_bytes=VMEM_BYTES),
    )(slots, query_rows, key_group, value_group, logsum, mixed, mixed_grad)


def pack_rows(pieces, width):
    blocks = []
    for piece in pieces:
        for start in range(0, piece.shape[1], width):
            blocks.append(piece[:, start : start + width])
    return blocks


def pack_vectors(pieces, width):
    joined = jnp.concatenate(pieces)
    count = -(-joined.shape[0] // width)
    return jnp.pad(joined, (0, count * width - joined.shape[0])).reshape(count, width)


def joined(pieces, axis):
    return pieces[0] if len(pieces) == 1 else jnp.concatenate(pieces, axis=axis)


def shards(
    inputs,
    cotangent,
    block_segment,
    segment_parent,
    query_weight,
    key_weight,
    value_weight,
    output_weight,
    gate_weight,
    gate_bias,
    up_weight,
    up_bias,
    down_weight,
    down_bias,
    carry_weight,
    carry_bias,
    first_gain,
    first_shift,
    second_gain,
    second_shift,
):
    width = inputs.shape[1]
    devices = lax.axis_size(BOTH)
    block_count = inputs.shape[0] // BLK
    group_blocks = block_segment.shape[0]

    vectors = (gate_bias, up_bias, down_bias, carry_bias, first_gain, first_shift, second_gain, second_shift)
    early = pack_rows((query_weight, key_weight, value_weight, gate_weight), width)
    late = pack_rows((output_weight, up_weight, down_weight, carry_weight), width)
    early = jnp.concatenate(early + [pack_vectors(vectors, width)])
    late = jnp.concatenate(late)
    early = jnp.pad(early, ((0, -early.shape[0] % 16), (0, 0)))
    early_rows = lax.all_gather(early, BOTH)
    input_group = lax.all_gather(inputs, "seq", axis=0, tiled=True)
    late_rows = lax.all_gather(late, BOTH)

    def take(source, start, piece):
        rows = piece.shape[0]
        parts = piece.shape[1] // width
        blocks = [
            source[:, start + part * rows : start + (part + 1) * rows].reshape(devices * rows, width)
            for part in range(parts)
        ]
        return (jnp.concatenate(blocks, axis=1) if parts > 1 else blocks[0]), start + parts * rows

    place = 0
    full_query, place = take(early_rows, place, query_weight)
    full_key, place = take(early_rows, place, key_weight)
    full_value, place = take(early_rows, place, value_weight)
    full_gate, place = take(early_rows, place, gate_weight)
    vector_rows = early_rows[:, place : place + -(-sum(v.shape[0] for v in vectors) // width)].reshape(devices, -1)
    full_vectors = []
    start = 0
    for vector in vectors:
        piece = vector_rows[:, start : start + vector.shape[0]].reshape(-1)
        full_vectors.append(piece.astype(jnp.float32))
        start += vector.shape[0]
    gate_b, up_b, down_b, carry_b, gain_one, shift_one, gain_two, shift_two = full_vectors
    place = 0
    full_output, place = take(late_rows, place, output_weight)
    full_up, place = take(late_rows, place, up_weight)
    full_down, place = take(late_rows, place, down_weight)
    full_carry, place = take(late_rows, place, carry_weight)

    own_start = lax.axis_index("seq") * block_count
    own_segments = lax.dynamic_slice_in_dim(block_segment, own_start, block_count)
    ancestor_slot, usable = ancestor_slots(block_segment, segment_parent, own_segments)
    slots = jnp.concatenate(
        [ancestor_slot, jnp.sum(usable, axis=-1, keepdims=True, dtype=jnp.int32)], axis=-1
    )

    values_in = inputs.astype(jnp.float32)
    normed_low = normalize(values_in, gain_one, shift_one).astype(jnp.bfloat16)
    query_low = (matmul(normed_low, full_query).astype(jnp.bfloat16) * (HD ** (-0.5))).astype(jnp.bfloat16)
    gate_open = jax.nn.sigmoid(matmul(normed_low, full_gate) + gate_b)
    normed_group = normalize(input_group.astype(jnp.float32), gain_one, shift_one).astype(jnp.bfloat16)
    key_group = matmul(normed_group, full_key).astype(jnp.bfloat16)
    value_group = matmul(normed_group, full_value).astype(jnp.bfloat16)

    cuts = max(1, group_blocks // 40)
    heads = [slice(cut * width // cuts, (cut + 1) * width // cuts) for cut in range(cuts)]
    forward = [
        attend(slots, query_low[:, cols], key_group[:, cols], value_group[:, cols]) for cols in heads
    ]
    attended_low = joined([mixed for mixed, logsum in forward], 1)

    branch = matmul(attended_low, full_output)
    middle = values_in + gate_open * branch
    normed_second = normalize(middle, gain_two, shift_two).astype(jnp.bfloat16)
    up_pre = matmul(normed_second, full_up) + up_b
    up_sigmoid = jax.nn.sigmoid(up_pre)
    hidden_low = (up_pre * up_sigmoid).astype(jnp.bfloat16)
    update = matmul(hidden_low, full_down) + down_b
    carry_open = jax.nn.sigmoid(matmul(normed_second, full_carry) + carry_b)
    output = (middle + carry_open * update).astype(jnp.bfloat16)

    grad_out = cotangent.astype(jnp.float32)
    update_grad = (carry_open * grad_out).astype(jnp.bfloat16)
    carry_pre_grad = (grad_out * update * carry_open * (1.0 - carry_open)).astype(jnp.bfloat16)
    grad_down = inner_rows(hidden_low, update_grad)
    grad_down_bias = column_sums(update_grad)
    grad_carry = inner_rows(normed_second, carry_pre_grad)
    grad_carry_bias = column_sums(carry_pre_grad)
    silu_slope = up_sigmoid * (1.0 + up_pre * (1.0 - up_sigmoid))
    up_pre_grad = (against(update_grad, full_down) * silu_slope).astype(jnp.bfloat16)
    grad_up = inner_rows(normed_second, up_pre_grad)
    grad_up_bias = column_sums(up_pre_grad)
    second_norm_grad = against(up_pre_grad, full_up) + against(carry_pre_grad, full_carry)
    second_pull = jax.vjp(normalize, middle, gain_two, shift_two)[1]
    middle_part, grad_second_gain, grad_second_shift = second_pull(second_norm_grad)
    middle_grad = grad_out + middle_part

    def spread(grad, piece):
        rows = piece.shape[0]
        return [
            grad[:, start : start + width].astype(jnp.bfloat16).reshape(devices, rows, width)
            for start in range(0, grad.shape[1], width)
        ]

    def own(summed, start, piece):
        rows = piece.shape[0]
        parts = piece.shape[1] // width
        blocks = [summed[start + part * rows : start + (part + 1) * rows] for part in range(parts)]
        return (jnp.concatenate(blocks, axis=1) if parts > 1 else blocks[0]), start + parts * rows

    first_pack = jnp.concatenate(
        spread(grad_up, up_weight) + spread(grad_down, down_weight) + spread(grad_carry, carry_weight), axis=1
    )
    first_sum = lax.psum_scatter(first_pack, BOTH, scatter_dimension=0, tiled=True)[0].astype(jnp.float32)

    branch_grad = (gate_open * middle_grad).astype(jnp.bfloat16)
    gate_pre_grad = (middle_grad * branch * gate_open * (1.0 - gate_open)).astype(jnp.bfloat16)
    grad_output = inner_rows(attended_low, branch_grad)
    grad_gate = inner_rows(normed_low, gate_pre_grad)
    grad_gate_bias = column_sums(gate_pre_grad)
    attended_grad = against(branch_grad, full_output).astype(jnp.bfloat16)

    backward = [
        attend_backward(
            slots,
            query_low[:, cols],
            key_group[:, cols],
            value_group[:, cols],
            logsum,
            attended_low[:, cols],
            attended_grad[:, cols],
        )
        for cols, (mixed, logsum) in zip(heads, forward)
    ]
    query_rows_grad = joined([query_part for query_part, sums in backward], 1)
    part = width // cuts
    sums = backward[0][1]
    if cuts > 1:
        sums = jnp.concatenate([sums[:part] for _, sums in backward] + [sums[part:] for _, sums in backward])

    both_weight = jnp.concatenate([full_key, full_value], axis=1)
    shared_grad = lax.dot_general(
        sums, both_weight, (((0,), (1,)), ((), ())), preferred_element_type=jnp.float32
    ).astype(jnp.bfloat16)
    shared_sum = lax.psum_scatter(shared_grad, "seq", scatter_dimension=0, tiled=True).astype(jnp.float32)
    grad_both = matmul(sums, normed_group)
    grad_key = jnp.transpose(grad_both[:width])
    grad_value = jnp.transpose(grad_both[width:])
    grad_query = inner_rows(normed_low, query_rows_grad)
    first_norm_grad = (
        against(query_rows_grad, full_query) + shared_sum + against(gate_pre_grad, full_gate)
    )
    first_pull = jax.vjp(normalize, values_in, gain_one, shift_one)[1]
    input_part, grad_first_gain, grad_first_shift = first_pull(first_norm_grad)
    input_grad = middle_grad + input_part

    vector_grads = (
        grad_gate_bias,
        grad_up_bias,
        grad_down_bias,
        grad_carry_bias,
        grad_first_gain,
        grad_first_shift,
        grad_second_gain,
        grad_second_shift,
    )
    vector_pack = jnp.concatenate([grad.reshape(devices, -1) for grad in vector_grads], axis=1)
    count = -(-vector_pack.shape[1] // width)
    vector_pack = jnp.pad(vector_pack, ((0, 0), (0, count * width - vector_pack.shape[1])))
    second_pack = (
        spread(grad_query, query_weight)
        + spread(grad_key, key_weight)
        + spread(grad_value, value_weight)
        + spread(grad_output, output_weight)
        + spread(grad_gate, gate_weight)
        + [vector_pack.astype(jnp.bfloat16).reshape(devices, count, width)]
    )
    second_pack = jnp.concatenate(second_pack, axis=1)
    second_pack = jnp.pad(second_pack, ((0, 0), (0, -second_pack.shape[1] % 16), (0, 0)))
    second_sum = lax.psum_scatter(second_pack, BOTH, scatter_dimension=0, tiled=True)[0].astype(jnp.float32)

    place = 0
    own_up, place = own(first_sum, place, up_weight)
    own_down, place = own(first_sum, place, down_weight)
    own_carry, place = own(first_sum, place, carry_weight)
    place = 0
    own_query, place = own(second_sum, place, query_weight)
    own_key, place = own(second_sum, place, key_weight)
    own_value, place = own(second_sum, place, value_weight)
    own_output, place = own(second_sum, place, output_weight)
    own_gate, place = own(second_sum, place, gate_weight)
    own_vectors = second_sum[place : place + count].reshape(-1)
    vector_out = []
    start = 0
    for vector in vectors:
        vector_out.append(own_vectors[start : start + vector.shape[0]])
        start += vector.shape[0]
    gate_bg, up_bg, down_bg, carry_bg, gain_one_g, shift_one_g, gain_two_g, shift_two_g = vector_out
    return (
        output,
        input_grad,
        own_query,
        own_key,
        own_value,
        own_output,
        own_gate,
        gate_bg,
        own_up,
        up_bg,
        own_down,
        down_bg,
        own_carry,
        carry_bg,
        gain_one_g,
        shift_one_g,
        gain_two_g,
        shift_two_g,
    )


def solution(mesh):
    rows = P(BOTH, None)
    line = P(BOTH)
    matrix_or_line = (rows,) * 5 + (line, rows, line, rows, line, rows) + (line,) * 5
    return jax.shard_map(
        shards,
        mesh=mesh,
        in_specs=(rows, rows, P("dp"), P("dp")) + matrix_or_line,
        out_specs=(rows, rows) + matrix_or_line,
        check_vma=False,
    )
```

time: 2130 us -> 632 us (0.30)
  waiting for transfers between devices: 1130 us -> 423 us
  blocking collectives: 505 us -> 0 us
  local copies, waits for them, and re-layouts: 174 us -> 51.6 us
  matrix products: 179 us -> 61.9 us
  other arithmetic: 93.8 us -> 19.3 us
  Pallas kernels: 0 us -> 48.6 us
    reduce_scatter x10 -> x2, waiting for transfers between devices: 1120 us -> 200 us  [the longest x1 101 us: shards(): lax.psum_scatter(first_pack, BOTH, scatter_dimension=0, tiled=True)[0]]
    all_gather x6 -> x0, blocking collectives: 423 us -> none  [the longest x1 74 us: shards(): lax.all_gather(output_weight, ('dp', 'seq'), axis=0, tiled=True)]
    all_gather x4 -> x3, waiting for transfers between devices: 0.03 us -> 157 us  [the longest x1 80.6 us: shards(): input_group = lax.all_gather(inputs, 'seq', axis=0, tiled=True)]
    dot_general x56 -> x1, matrix products: 120 us -> 10.2 us  [shards(): lax.dot_general(sums, both_weight, (((0,), (1,)), ((), ())), preferred_el...]
    another operation x8 -> x0, local copies, waits for them, and re-layouts: 95.7 us -> none  [the longest x2 42.4 us: shards(): merge_heads(value_parts).reshape(-1, BLK, model_width)]
    unnamed x2 -> x0, blocking collectives: 81.6 us -> none
    unnamed x14 -> x7, waiting for transfers between devices: 1.4 us -> 66.1 us
    scatter-add x2 -> x0, other arithmetic: 63.6 us -> none  [the longest x1 31.9 us: shards(): value_sums = jnp.zeros((group_blocks, BLK, model_width), jnp.float32).at[...]
  transfers between devices with their start and end apart: 14 -> 6, of which waited for: 9 -> 6; matrix products, arithmetic and copies ran while one was open for 11% -> 14% of each run, Pallas kernels for 0% -> 3%
where the time goes in v1:
time: 632 us; the launch traced here: 620 us
  waiting for transfers between devices  423 us (67%)
  matrix products  61.9 us (10%)
  local copies, waits for them, and re-layouts  51.6 us (8%)
  Pallas kernels  48.6 us (8%)
  other arithmetic  19.3 us (3%)
  between operations  15.1 us (2%)
    reduce_scatter x1, waiting for transfers between devices, shards(): lax.psum_scatter(first_pack, BOTH, scatter_dimension=0, tiled=True)[0]  101 us
    reduce_scatter x1, waiting for transfers between devices, shards(): lax.psum_scatter(second_pack, BOTH, scatter_dimension=0, tiled=True)[0]  99.2 us
    all_gather x1, waiting for transfers between devices, shards(): input_group = lax.all_gather(inputs, 'seq', axis=0, tiled=True)  80.6 us
    unnamed x7, waiting for transfers between devices  66.1 us
    all_gather x1, waiting for transfers between devices, shards(): early_rows = lax.all_gather(early, BOTH)  46.8 us
    dot_general x9, matrix products, matmul(): return jnp.dot(left_side, right_side, preferred_element_type=jnp.float32)  32.6 us
    all_gather x1, waiting for transfers between devices, shards(): late_rows = lax.all_gather(late, BOTH)  29.9 us
    pallas_call x1, Pallas kernels, attend_backward(): pl.pallas_call(backward_kernel, out_shape=(jax.ShapeDtypeStruct((rows, wi...  29.7 us
  transfers between devices with their start and end apart: 6, of which 6 were waited for; matrix products, arithmetic and copies ran while one was open for 14% of the time, Pallas kernels for 3%

profile of v1, /device:TPU:28, one launch (start us, length us, event | category | flops | bytes accessed | tf_op | source)
XLA Modules:
  0.0 620.4 jit_solution(2406811283074500049)
XLA Ops:
  8.0 5.4 concatenate.31
  27.7 46.8 %all-gather.8.cloned.1.call-done = bf16[2560,512]{1,0:T(8,128)(2,1)} async-done(((bf16[80,512]{1,0:T(8,128)(2,1)}), bf16[2560,512]{1,0:T(8,128)(2,1)}) %all-gather.8.cloned.1.call-update) | async-done | bytes 2621456 | tf_op jit(solution)/shard_map/all_gather | solution.py:279
  74.4 1.0 slice.287
  76.2 2.6 fusion.58
  78.8 1.6 fusion.29.query_ref
  80.4 80.6 %all-gather.6.cloned.1.call-done = bf16[5120,512]{1,0:T(8,128)(2,1)} async-done(((bf16[640,512]{1,0:T(8,128)(2,1)}), bf16[5120,512]{1,0:T(8,128)(2,1)}) %all-gather.6.cloned.1.call-update) | async-done | bytes 5242896 | tf_op jit(solution)/shard_map/all_gather | solution.py:280
  161.0 3.4 convert_reduce_fusion
  165.1 3.2 fusion.2
  168.3 5.9 convolution_convert_fusion.1.value_ref
  174.2 5.8 convolution_convert_fusion.2.key_ref
  180.0 18.9 %shard_map.331 = (bf16[640,512]{1,0:T(8,128)(2,1)}, f32[640,128]{1,0:T(8,128)}) custom-call(s32[5,11]{1,0:T(8,128)} %pad_add_fusion.slots_ref, bf16[640,512]{1,0:T(8,128)(2,1)} %fusion.29.query_ref, bf16[5120,512]{1,0:T(8,128)(2,1)} %convolution_convert_fusion.2.key_ref, bf16[5120,512]{1,0:T(8,128)(2,1)} %convolution_convert_fusion.1.value_ref), custom_call_target="tpu_custom_call" | custom-call | tf_op jit(solution)/shard_map/pallas_call | solution.py:189
  198.9 29.9 %all-gather.10.cloned.1.call-done = bf16[5120,512]{1,0:T(8,128)(2,1)} async-done(((bf16[160,512]{1,0:T(8,128)(2,1)}), bf16[5120,512]{1,0:T(8,128)(2,1)}) %all-gather.10.cloned.1.call-update) | async-done | bytes 5242896 | tf_op jit(solution)/shard_map/all_gather | solution.py:281
  228.9 1.7 slice.305
  230.6 2.2 fusion.57
  233.5 0.9 fusion.56
  235.0 2.4 multiply_convert_fusion.1
  237.4 1.9 convolution_add_fusion.5
  239.3 1.1 fusion.50
  240.5 3.1 fusion.61
  243.6 1.8 fusion.33
  245.5 1.0 multiply_reduce_fusion
  246.5 1.4 fusion.55
  248.1 1.4 convolution_convert_fusion.6.mixed_grad_ref
  249.5 29.7 %shard_map.332 = (bf16[640,512]{1,0:T(8,128)(2,1)}, bf16[1024,5120]{1,0:T(8,128)(2,1)}) custom-call(s32[5,11]{1,0:T(8,128)} %pad_add_fusion.slots_ref, bf16[640,512]{1,0:T(8,128)(2,1)} %fusion.29.query_ref, bf16[5120,512]{1,0:T(8,128)(2,1)} %convolution_convert_fusion.2.key_ref, bf16[5120,512]{1,0:T(8,128)(2,1)} %convolution_convert_fusion.1.value_ref, ...), custom_call_target="tpu_custom_call" | custom-call | tf_op jit(solution)/shard_map/pallas_call | solution.py:209
  279.2 10.2 %convolution_convert_fusion = bf16[5120,512]{1,0:T(8,128)(2,1)} fusion(bf16[1024,5120]{1,0:T(8,128)(2,1)} %get-tuple-element.25, bf16[512,512]{1,0:T(8,128)(2,1)S(1)} %bitcast.155, bf16[512,512]{1,0:T(8,128)(2,1)} %bitcast.156), kind=kOutput, calls=%fused_computation.8 | convolution fusion | flops 5373427712 | bytes 16777216 | tf_op jit(solution)/shard_map/dot_general | solution.py:403
  289.5 3.8 convolution_convert_fusion.4
  294.3 0.9 constant_dynamic-update-slice_fusion.21
  296.9 1.9 convolution_convert_fusion.3
  298.8 1.6 constant_dynamic-update-slice_fusion.18
  302.3 2.2 fusion.54
  304.8 1.7 convolution_convert_fusion.11
  306.6 0.9 constant_dynamic-update-slice_fusion.16
  307.5 12.4 %convolution_convert_fusion.5 = bf16[1024,512]{0,1:T(8,128)(2,1)} fusion(bf16[1024,5120]{1,0:T(8,128)(2,1)} %get-tuple-element.25, bf16[5120,512]{1,0:T(8,128)(2,1)} %all-gather.6.cloned.1.call-done, f32[512]{0:T(512)S(1)} %reshape.350, f32[512]{0:T(512)S(1)} %reshape.349, f32[5120]{0:T(1024)S(1)} %add_rsqrt_fusion, f32[5120]{0:T(1024)S(1)} %broadcast_multiply_fusion), kind=kOutput, calls=%fused_computation.29 | convolution fusion | flops 5384962048 | bytes 16822272 | tf_op jit(solution)/shard_map/dot_general | solution.py:28
  319.9 1.3 fusion.60
  321.2 0.9 constant_dynamic-update-slice_fusion.15
  322.1 0.9 constant_dynamic-update-slice_fusion.14
  325.1 0.9 constant_dynamic-update-slice_fusion.12
  326.0 65.3 %reduce-scatter.10.cloned.1.call-done = bf16[640,512]{1,0:T(8,128)(2,1)} async-done(((bf16[5120,512]{1,0:T(8,128)(2,1)}), bf16[640,512]{1,0:T(8,128)(2,1)}) %reduce-scatter.10.cloned.1.call-update) | async-done | bytes 655376
  391.3 1.4 copy.159
  392.7 1.8 convolution_add_fusion.2
  396.8 3.9 pad.20
  400.7 2.2 copy.150
  402.9 100.8 %reduce-scatter.8.cloned.1.call-done = bf16[1,144,512]{2,1,0:T(8,128)(2,1)} async-done(((bf16[32,144,512]{2,1,0:T(8,128)(2,1)}), bf16[1,144,512]{2,1,0:T(8,128)(2,1)}) %reduce-scatter.8.cloned.1.call-update) | async-done | bytes 147472 | tf_op jit(solution)/shard_map/reduce_scatter | solution.py:375
  503.7 1.0 convert_element_type.247
  506.6 1.7 add_add_fusion.2
  508.3 2.8 copy.151
  511.1 99.2 %reduce-scatter.6.cloned.1.call-done = bf16[1,96,512]{2,1,0:T(8,128)(2,1)} async-done(((bf16[32,96,512]{2,1,0:T(8,128)(2,1)}), bf16[1,96,512]{2,1,0:T(8,128)(2,1)}) %reduce-scatter.6.cloned.1.call-update) | async-done | bytes 98320 | tf_op jit(solution)/shard_map/reduce_scatter | solution.py:441
  610.3 0.9 convert_bitcast_fusion
  (182 shorter events, 31.1 us)
Async XLA Ops:
  7.2 15.1 %copy-start.9 = (bf16[640,512]{1,0:T(8,128)(2,1)S(1)}, bf16[640,512]{1,0:T(8,128)(2,1)}, u32[]{:S(2)}) copy-start(bf16[640,512]{1,0:T(8,128)(2,1)} %param.20) | copy-start | bytes 1966084
  7.2 14.4 %copy-start.23 = (bf16[16,512]{1,0:T(8,128)(2,1)S(1)}, bf16[16,512]{1,0:T(8,128)(2,1)}, u32[]{:S(2)}) copy-start(bf16[16,512]{1,0:T(8,128)(2,1)} %param.34) | copy-start | bytes 49156
  7.2 67.2 %all-gather.8.cloned.1.call-start = ((), (), s32[]{:S(2)}) async-start(), calls=%async_computation.6 | async-start | bytes 2703360 | tf_op jit(solution)/shard_map/all_gather | solution.py:279
  16.3 6.4 %copy-start.24 = (s32[40]{0:T(128)S(1)}, s32[40]{0:T(128)}, u32[]{:S(2)}) copy-start(s32[40]{0:T(128)} %param.22) | copy-start | bytes 484
  16.3 6.4 %copy-start.25 = (s32[40]{0:T(128)S(1)}, s32[40]{0:T(128)}, u32[]{:S(2)}) copy-start(s32[40]{0:T(128)} %param.23) | copy-start | bytes 484
  16.3 9.9 %copy-start.14 = (bf16[640,512]{1,0:T(8,128)(2,1)S(1)}, bf16[640,512]{1,0:T(8,128)(2,1)}, u32[]{:S(2)}) copy-start(bf16[640,512]{1,0:T(8,128)(2,1)} %param.21) | copy-start | bytes 1966084
  16.3 144.7 %all-gather.6.cloned.1.call-start = ((), (), s32[]{:S(2)}) async-start(), calls=%async_computation.3 | async-start | bytes 5898240 | tf_op jit(solution)/shard_map/all_gather | solution.py:280
  17.1 211.8 %all-gather.10.cloned.1.call-start = ((), (), s32[]{:S(2)}) async-start(), calls=%async_computation.7 | async-start | bytes 5406720 | tf_op jit(solution)/shard_map/all_gather | solution.py:281
  21.6 0.7 copy-start.22
  22.3 369.0 %reduce-scatter.10.cloned.1.call-start = ((), (), s32[]{:S(2)}) async-start(), calls=%async_computation.8 | async-start | bytes 5898240
  26.5 275.8 %copy-start.1 = (bf16[640,512]{0,1:T(8,128)(2,1)}, bf16[640,512]{0,1:T(8,128)(2,1)S(1)}, u32[]{:S(2)}) copy-start(bf16[640,512]{0,1:T(8,128)(2,1)S(1)} %copy.143) | copy-start | bytes 1966084
  78.8 1.6 copy-start.12
  78.8 89.5 %copy-start.19 = (bf16[32,16,512]{2,1,0:T(8,128)(2,1)}, bf16[32,16,512]{2,1,0:T(8,128)(2,1)S(1)}, u32[]{:S(2)}) copy-start(bf16[32,16,512]{2,1,0:T(8,128)(2,1)S(1)} %get-tuple-element.141) | copy-start | bytes 1572868
  78.8 154.7 %copy-start.10 = (bf16[32,16,512]{2,1,0:T(8,128)(2,1)}, bf16[32,16,512]{2,1,0:T(8,128)(2,1)S(1)}, u32[]{:S(2)}) copy-start(bf16[32,16,512]{2,1,0:T(8,128)(2,1)S(1)} %get-tuple-element.144) | copy-start | bytes 1572868
  161.0 4.0 copy-start
  168.3 5.9 copy-start.21
  230.6 2.2 copy-start.5
  233.5 1.1 copy-start.3
  234.6 13.3 %copy-start.4 = (f32[640,512]{0,1:T(8,128)}, f32[640,512]{0,1:T(8,128)S(1)}, u32[]{:S(2)}) copy-start(f32[640,512]{0,1:T(8,128)S(1)} %get-tuple-element.180) | copy-start | bytes 3932164
  235.0 4.3 copy-start.17
  237.4 1.9 copy-start.27
  240.5 3.2 copy-start.29
  243.6 1.8 copy-start.26
  248.1 1.4 copy-start.15
  249.5 29.7 %copy-start.20 = (bf16[32,16,512]{2,1,0:T(8,128)(2,1)S(1)}, bf16[32,16,512]{2,1,0:T(8,128)(2,1)}, u32[]{:S(2)}) copy-start(bf16[32,16,512]{2,1,0:T(8,128)(2,1)} %copy-done.19) | copy-start | bytes 1572868
  289.4 214.2 %reduce-scatter.8.cloned.1.call-start = ((), (), s32[]{:S(2)}) async-start(), calls=%async_computation.5 | async-start | bytes 4866048 | tf_op jit(solution)/shard_map/reduce_scatter | solution.py:375
  293.4 3.5 copy-start.30
  294.3 2.6 copy-start.28
  298.8 1.6 copy-start.18
  301.8 308.5 %reduce-scatter.6.cloned.1.call-start = ((), (), s32[]{:S(2)}) async-start(), calls=%async_computation.4 | async-start | bytes 3244032 | tf_op jit(solution)/shard_map/reduce_scatter | solution.py:441
  304.5 20.0 %copy-start.7 = (bf16[640,512]{0,1:T(8,128)(2,1)}, bf16[640,512]{0,1:T(8,128)(2,1)S(1)}, u32[]{:S(2)}) copy-start(bf16[640,512]{0,1:T(8,128)(2,1)S(1)} %get-tuple-element.128) | copy-start | bytes 1966084
  321.2 1.8 copy-start.6
  321.2 1.8 copy-start.16
  325.1 67.6 %copy-start.13 = (bf16[32,16,512]{2,1,0:T(8,128)(2,1)S(1)}, bf16[32,16,512]{2,1,0:T(8,128)(2,1)}, u32[]{:S(2)}) copy-start(bf16[32,16,512]{2,1,0:T(8,128)(2,1)} %copy-done.12) | copy-start | bytes 1572868
  392.7 1.8 copy-start.8
  392.7 1.8 copy-start.11
  503.7 3.0 copy-start.2
Sparse Core Ops, SparseCore 0:
  16.4 57.9 all-gather.7
  76.6 84.3 all-gather.5
  164.4 64.3 all-gather.9
  289.6 101.6 reduce-scatter.9
  396.6 106.9 reduce-scatter.7
  509.8 100.4 reduce-scatter.5

commit v2 on v1

--- a/solution.py
+++ b/solution.py
@@ -124,22 +124,31 @@
 def backward_kernel(
     slots_ref,
     query_ref,
-    key_ref,
-    value_ref,
+    key_source,
+    value_source,
     logsum_ref,
     mixed_ref,
     mixed_grad_ref,
-    query_grad_ref,
-    sums_ref,
-    key_here,
-    value_here,
-    bias_ref,
-    key_sums,
-    value_sums,
+    normed_source,
+    weight_ref,
+    *refs,
 ):
+    query_grad_ref, grads_ref, lanes_ref = refs[:3]
+    shared_refs = refs[3:-9]
+    key_ref, value_ref, normed_ref, key_here, value_here, bias_ref, key_sums, value_sums, copies = refs[-9:]
     width = query_ref.shape[1]
+    fetches = [
+        pltpu.make_async_copy(source, target, copies.at[index])
+        for index, (source, target) in enumerate(
+            ((key_source, key_ref), (value_source, value_ref), (normed_source, normed_ref))
+        )
+    ]
+    for fetch in fetches:
+        fetch.start()
     key_sums[...] = jnp.zeros_like(key_sums)
     value_sums[...] = jnp.zeros_like(value_sums)
+    fetches[0].wait()
+    fetches[1].wait()
 
     def one_slot(slot, carry):
         rows = pl.ds(pl.multiple_of(slot * BLK, BLK), BLK)
@@ -172,8 +181,32 @@
         return carry
 
     lax.fori_loop(0, query_ref.shape[0] // BLK, one_slot, 0)
-    sums_ref[:width, :] = key_sums[...].astype(jnp.bfloat16)
-    sums_ref[width:, :] = value_sums[...].astype(jnp.bfloat16)
+
+    fetches[2].wait()
+    piece = key_sums.shape[1] // len(shared_refs)
+    for index in range(len(shared_refs)):
+        here = slice(index * piece, (index + 1) * piece)
+        shared = None
+        for part, part_sums in enumerate((key_sums, value_sums)):
+            lines = slice(part * width, (part + 1) * width)
+            block = part_sums[:, here]
+            tiles = [block[:, start : start + BLK] for start in range(0, piece, BLK)]
+            lane_sums = functools.reduce(lambda left, right: left + right, tiles)
+            low = block.astype(jnp.bfloat16)
+            product = matmul(weight_ref[:, lines], low)
+            shared = product if shared is None else shared + product
+            grad = matmul(low, normed_ref[here, :])
+            if index == 0:
+                grads_ref[lines, :] = grad
+                lanes_ref[lines, :] = lane_sums
+            else:
+                grads_ref[lines, :] += grad
+                lanes_ref[lines, :] += lane_sums
+        shared_refs[index][...] = shared.astype(jnp.bfloat16)
+
+
+def about(cost):
+    return pl.CostEstimate(flops=int(cost * 1e9), bytes_accessed=int(cost * 1e6), transcendentals=0)
 
 
 def in_vmem():
@@ -188,6 +221,7 @@
     rows, width = query_rows.shape
     return pl.pallas_call(
         forward_kernel,
+        cost_estimate=about(18),
         out_shape=(
             jax.ShapeDtypeStruct((rows, width), jnp.bfloat16),
             jax.ShapeDtypeStruct((rows, PAIR), jnp.float32),
@@ -203,40 +237,305 @@
     )(slots, query_rows, key_group, value_group)
 
 
-def attend_backward(slots, query_rows, key_group, value_group, logsum, mixed, mixed_grad):
+def attend_backward(slots, query_rows, key_group, value_group, logsum, mixed, mixed_grad, normed_group, both_weight):
     rows, width = query_rows.shape
-    keys = key_group.shape[0]
+    keys, model_width = normed_group.shape
+    pieces = keys // rows
+
+    anywhere = pl.BlockSpec(memory_space=pl.ANY)
     return pl.pallas_call(
         backward_kernel,
+        cost_estimate=about(40),
         out_shape=(
             jax.ShapeDtypeStruct((rows, width), jnp.bfloat16),
-            jax.ShapeDtypeStruct((2 * width, keys), jnp.bfloat16),
-        ),
-        in_specs=[in_smem()] + [in_vmem()] * 6,
-        out_specs=(in_vmem(), in_vmem()),
+            jax.ShapeDtypeStruct((2 * width, model_width), jnp.float32),
+            jax.ShapeDtypeStruct((2 * width, BLK), jnp.float32),
+        )
+        + (jax.ShapeDtypeStruct((model_width, rows), jnp.bfloat16),) * pieces,
+        in_specs=[in_smem(), in_vmem(), anywhere, anywhere, in_vmem(), in_vmem(), in_vmem(), anywhere, in_vmem()],
+        out_specs=(in_vmem(),) * (3 + pieces),
         scratch_shapes=[
+            pltpu.VMEM((keys, width), jnp.bfloat16),
+            pltpu.VMEM((keys, width), jnp.bfloat16),
+            pltpu.VMEM((keys, model_width), jnp.bfloat16),
             pltpu.VMEM((DEPTH * BLK, width), jnp.bfloat16),
             pltpu.VMEM((DEPTH * BLK, width), jnp.bfloat16),
             pltpu.VMEM((2 * BLK, DEPTH * BLK), jnp.float32),
             pltpu.VMEM((width, keys), jnp.float32),
             pltpu.VMEM((width, keys), jnp.float32),
+            pltpu.SemaphoreType.DMA((3,)),
         ],
         compiler_params=pltpu.CompilerParams(vmem_limit_bytes=VMEM_BYTES),
-    )(slots, query_rows, key_group, value_group, logsum, mixed, mixed_grad)
-
-
-def pack_rows(pieces, width):
-    blocks = []
-    for piece in pieces:
-        for start in range(0, piece.shape[1], width):
-            blocks.append(piece[:, start : start + width])
-    return blocks
-
-
-def pack_vectors(pieces, width):
-    joined = jnp.concatenate(pieces)
-    count = -(-joined.shape[0] // width)
-    return jnp.pad(joined, (0, count * width - joined.shape[0])).reshape(count, width)
+    )(slots, query_rows, key_group, value_group, logsum, mixed, mixed_grad, normed_group, both_weight)
+
+
+def project_kernel(pieces, vectors_ref, key_weight_ref, value_weight_ref, refs):
+    normed_ref, key_ref, value_ref = refs[-3:]
+    gain = vectors_ref[GAIN_ONE : GAIN_ONE + 1, :]
+    shift = vectors_ref[SHIFT_ONE : SHIFT_ONE + 1, :]
+    for index, piece in enumerate(pieces):
+        rows = slice(index * piece.shape[0], (index + 1) * piece.shape[0])
+        normed = normalize(piece[...].astype(jnp.float32), gain, shift).astype(jnp.bfloat16)
+        normed_ref[rows, :] = normed
+        key_ref[rows, :] = matmul(normed, key_weight_ref[...]).astype(jnp.bfloat16)
+        value_ref[rows, :] = matmul(normed, value_weight_ref[...]).astype(jnp.bfloat16)
+
+
+def project(pieces, vectors, key_weight, value_weight, group_rows, step, carried):
+    count = len(pieces)
+    rows, width = pieces[0].shape
+
+    def body(*refs):
+        project_kernel(refs[:count], *refs[count : count + 3], refs)
+
+    block = pl.BlockSpec((count * rows, width), lambda index: (step, 0))
+    whole = jax.ShapeDtypeStruct((group_rows, width), jnp.bfloat16)
+    extra = [] if carried is None else list(carried)
+    return pl.pallas_call(
+        body,
+        cost_estimate=about(4),
+        grid=(1,),
+        out_shape=(whole,) * 3,
+        in_specs=[in_vmem()] * (count + 3) + [pl.BlockSpec(memory_space=pl.ANY)] * len(extra),
+        out_specs=(block,) * 3,
+        input_output_aliases={count + 3 + index: index for index in range(len(extra))},
+        compiler_params=pltpu.CompilerParams(vmem_limit_bytes=VMEM_BYTES),
+    )(*pieces, vectors, key_weight, value_weight, *extra)
+
+
+class Axis:
+    def __init__(self, name, size, stride):
+        self.name = name
+        self.size = size
+        self.stride = stride
+
+    def position(self):
+        return lax.axis_index(self.name) // self.stride % self.size
+
+    def rotate(self, values, shift):
+        pairs = []
+        for index in range(lax.axis_size(self.name)):
+            here = index // self.stride % self.size
+            there = (here + shift) % self.size
+            pairs.append((index, index + (there - here) * self.stride))
+        return lax.ppermute(values, self.name, pairs)
+
+
+def axes():
+    seq = lax.axis_size("seq")
+    dp = lax.axis_size("dp")
+    along_z = 4 if seq % 4 == 0 else 1
+    cores = 2 if dp % 2 == 0 else 1
+    return (
+        Axis("seq", along_z, seq // along_z),
+        Axis("seq", seq // along_z, 1),
+        Axis("dp", dp // cores, cores),
+        Axis("dp", cores, 1),
+    )
+
+
+def relative_devices():
+    axis_z, axis_x, axis_y, axis_core = axes()
+
+    def place(axis, dim):
+        back = lax.broadcasted_iota(jnp.int32, (axis_core.size, axis_y.size, axis_x.size, axis_z.size), dim)
+        return (axis.position() - back + axis.size) % axis.size
+
+    dp_index = place(axis_y, 1) * axis_core.size + place(axis_core, 0)
+    seq_index = place(axis_z, 3) * axis_x.size + place(axis_x, 2)
+    return (dp_index * lax.axis_size("seq") + seq_index).reshape(-1)
+
+
+def add_low(left_side, right_side):
+    return (left_side.astype(jnp.float32) + right_side.astype(jnp.float32)).astype(jnp.bfloat16)
+
+
+def ring_scatter(entry, axis):
+    running = entry(axis.size - 1)
+    for back in range(axis.size - 1, 0, -1):
+        running = add_low(axis.rotate(running, -1), entry(back - 1))
+    return running
+
+
+def pair_scatter(keep, send, axis):
+    arrived = axis.rotate(send, -1)
+    return lambda index: add_low(arrived[index], keep[index])
+
+
+GATE_B, DOWN_B, CARRY_B, GAIN_ONE, SHIFT_ONE, GAIN_TWO, SHIFT_TWO, UP_B = range(8)
+VECTOR_ROWS = 16
+
+
+def pack_kernel(place_ref, *refs):
+    early_sources, late_sources, vector_refs, (early_ref, late_ref) = refs[:4], refs[4:8], refs[8:16], refs[16:]
+    width = early_ref.shape[1]
+    for target, sources in ((early_ref, early_sources), (late_ref, late_sources)):
+        start = 0
+        for source in sources:
+            rows = source.shape[0]
+            for column in range(0, source.shape[1], width):
+                target[start : start + rows, :] = source[:, column : column + width]
+                start += rows
+    block = jnp.zeros((VECTOR_ROWS, width), jnp.float32)
+    line = lax.broadcasted_iota(jnp.int32, block.shape, 0)
+    for index, source in enumerate(vector_refs):
+        count = source.shape[1]
+        feature = lax.broadcasted_iota(jnp.int32, (count, width), 0) + place_ref[0] * count
+        column = lax.broadcasted_iota(jnp.int32, (count, width), 1)
+        for part in range(count * place_ref.shape[0] // width):
+            spot = jnp.where(feature == column + part * width, jnp.float32(1.0), jnp.float32(0.0))
+            spread = matmul(source[...], spot.astype(jnp.bfloat16))
+            block += jnp.where(line == index + part, spread, jnp.float32(0.0))
+    early_ref[early_ref.shape[0] - VECTOR_ROWS :, :] = block.astype(jnp.bfloat16)
+
+
+def unpack_kernel(place_ref, mine_ref, other_ref, query_ref, key_ref, value_ref, gate_ref, vectors_ref):
+    half = mine_ref.shape[0]
+    rows = (mine_ref.shape[1] - VECTOR_ROWS) // 4
+    vectors = jnp.zeros(vectors_ref.shape, jnp.float32)
+    for index in range(2 * half):
+        source = (mine_ref if index < half else other_ref).at[index % half]
+        target = pl.ds(pl.multiple_of(place_ref[index] * rows, rows), rows)
+        for part, weight_ref in enumerate((query_ref, key_ref, value_ref, gate_ref)):
+            weight_ref[target, :] = source[part * rows : (part + 1) * rows, :]
+        vectors += source[4 * rows :, :].astype(jnp.float32)
+    vectors_ref[...] = vectors
+
+
+def unpack_late_kernel(
+    place_ref, line_ref, line_other_ref, plane_ref, plane_other_ref, output_ref, up_ref, down_ref, carry_ref
+):
+    half = line_ref.shape[0]
+    width = output_ref.shape[1]
+    rows = output_ref.shape[0] // (2 * half)
+    down_rows = down_ref.shape[0] // (2 * half)
+    for index in range(2 * half):
+        source = (line_ref if index < half else line_other_ref).at[index % half]
+        target = pl.ds(pl.multiple_of(place_ref[0, index] * rows, rows), rows)
+        output_ref[target, :] = source[:rows, :]
+        for part in range(up_ref.shape[1] // width):
+            up_ref[target, part * width : (part + 1) * width] = source[(part + 1) * rows : (part + 2) * rows, :]
+        source = (plane_ref if index < half else plane_other_ref).at[index % half]
+        target = pl.ds(pl.multiple_of(place_ref[1, index] * down_rows, down_rows), down_rows)
+        down_ref[target, :] = source[:down_rows, :]
+        target = pl.ds(pl.multiple_of(place_ref[1, index] * rows, rows), rows)
+        carry_ref[target, :] = source[down_rows:, :]
+
+
+def spread_rows(place_ref, grad_ref, keep_ref, send_ref, start, rows):
+    half = keep_ref.shape[0]
+    for index in range(2 * half):
+        source = pl.ds(pl.multiple_of(place_ref[index] * rows, rows), rows)
+        target = (keep_ref if index < half else send_ref).at[index % half]
+        target[start : start + rows, :] = grad_ref[source, :].astype(jnp.bfloat16)
+
+
+def first_grads_kernel(
+    place_ref,
+    hidden_ref,
+    update_grad_ref,
+    normed_second_ref,
+    up_pre_ref,
+    carry_pre_ref,
+    attended_ref,
+    branch_grad_ref,
+    normed_ref,
+    gate_pre_ref,
+    keep_ref,
+    send_ref,
+    up_grad,
+    down_grad,
+    square_grads,
+):
+    width = keep_ref.shape[2]
+    rows = width // (2 * keep_ref.shape[0])
+    start = 0
+    for part in range(up_pre_ref.shape[1] // width):
+        grad = up_grad.at[part]
+        grad[...] = inner_rows(normed_second_ref[...], up_pre_ref[:, part * width : (part + 1) * width])
+        spread_rows(place_ref, grad, keep_ref, send_ref, start, rows)
+        start += rows
+    for part in range(hidden_ref.shape[1] // width):
+        here = slice(part * width, (part + 1) * width)
+        down_grad[here, :] = inner_rows(hidden_ref[:, here], update_grad_ref[...])
+    down_rows = hidden_ref.shape[1] // (2 * keep_ref.shape[0])
+    spread_rows(place_ref, down_grad, keep_ref, send_ref, start, down_rows)
+    start += down_rows
+    pairs = ((normed_second_ref, carry_pre_ref), (attended_ref, branch_grad_ref), (normed_ref, gate_pre_ref))
+    for index, (left_ref, right_ref) in enumerate(pairs):
+        grad = square_grads.at[index]
+        grad[...] = inner_rows(left_ref[...], right_ref[...])
+        spread_rows(place_ref, grad, keep_ref, send_ref, start, rows)
+        start += rows
+
+
+def second_grads_kernel(
+    place_ref,
+    both_grads_ref,
+    normed_ref,
+    query_grad_ref,
+    gate_pre_ref,
+    lanes_ref,
+    query_weight_ref,
+    key_weight_ref,
+    value_weight_ref,
+    gate_weight_ref,
+    vectors_ref,
+    block_ref,
+    keep_ref,
+    send_ref,
+    grads,
+):
+    width = keep_ref.shape[2]
+    rows = width // (2 * keep_ref.shape[0])
+    grads[0] = inner_rows(normed_ref[...], query_grad_ref[...])
+    grads[1] = jnp.transpose(both_grads_ref[:width, :])
+    grads[2] = jnp.transpose(both_grads_ref[width:, :])
+    for index in range(3):
+        spread_rows(place_ref, grads.at[index], keep_ref, send_ref, index * rows, rows)
+    gate_grad = inner_rows(normed_ref[...], gate_pre_ref[...])
+
+    def line_sums(ref):
+        return jnp.sum(ref[...].astype(jnp.float32), axis=0, keepdims=True)
+
+    def as_line(column):
+        return jnp.transpose(jnp.broadcast_to(column, (width, BLK)))[:1, :]
+
+    lines = (
+        line_sums(query_grad_ref),
+        jnp.sum(jnp.transpose(lanes_ref[:width, :]), axis=0, keepdims=True),
+        jnp.sum(jnp.transpose(lanes_ref[width:, :]), axis=0, keepdims=True),
+        line_sums(gate_pre_ref),
+    )
+    weighted = jnp.zeros((width, width), jnp.float32)
+    shifted = jnp.zeros((width, width), jnp.float32)
+    weight_refs = (query_weight_ref, key_weight_ref, value_weight_ref, gate_weight_ref)
+    for weight_ref, line, grad in zip(weight_refs, lines, (grads[0], grads[1], grads[2], gate_grad)):
+        weight = weight_ref[...].astype(jnp.float32)
+        weighted += weight * grad
+        shifted += weight * line
+    shift_line = as_line(jnp.sum(shifted, axis=1, keepdims=True))
+    gain_line = (
+        as_line(jnp.sum(weighted, axis=1, keepdims=True)) - vectors_ref[SHIFT_ONE : SHIFT_ONE + 1, :] * shift_line
+    ) / vectors_ref[GAIN_ONE : GAIN_ONE + 1, :]
+    place = lax.broadcasted_iota(jnp.int32, block_ref.shape, 0)
+    block = jnp.where(place == GAIN_ONE, gain_line, block_ref[...])
+    block = jnp.where(place == SHIFT_ONE, shift_line, block).astype(jnp.bfloat16)
+    for index in range(keep_ref.shape[0]):
+        keep_ref[index, 3 * rows :, :] = block
+        send_ref[index, 3 * rows :, :] = block
+
+
+def local_call(kernel, cost, outs, smem, args, scratch=()):
+    return pl.pallas_call(
+        kernel,
+        cost_estimate=about(cost),
+        out_shape=outs,
+        in_specs=[in_smem()] + [in_vmem()] * len(args),
+        out_specs=jax.tree.map(lambda out: in_vmem(), outs),
+        scratch_shapes=list(scratch),
+        compiler_params=pltpu.CompilerParams(vmem_limit_bytes=VMEM_BYTES),
+    )(smem, *args)
 
 
 def joined(pieces, axis):
@@ -270,15 +569,19 @@
     block_count = inputs.shape[0] // BLK
     group_blocks = block_segment.shape[0]
 
-    vectors = (gate_bias, up_bias, down_bias, carry_bias, first_gain, first_shift, second_gain, second_shift)
-    early = pack_rows((query_weight, key_weight, value_weight, gate_weight), width)
-    late = pack_rows((output_weight, up_weight, down_weight, carry_weight), width)
-    early = jnp.concatenate(early + [pack_vectors(vectors, width)])
-    late = jnp.concatenate(late)
-    early = jnp.pad(early, ((0, -early.shape[0] % 16), (0, 0)))
-    early_rows = lax.all_gather(early, BOTH)
-    input_group = lax.all_gather(inputs, "seq", axis=0, tiled=True)
-    late_rows = lax.all_gather(late, BOTH)
+    axis_z, axis_x, axis_y, axis_core = axes()
+    rows_each = query_weight.shape[0]
+    sizes = (axis_z.size, axis_x.size, axis_y.size, axis_core.size)
+    direct = sizes == (4, 2, 2, 2) and rows_each % 16 == 0
+    places = relative_devices()
+    device = lax.axis_index(BOTH)
+    vectors = (gate_bias, down_bias, carry_bias, first_gain, first_shift, second_gain, second_shift, up_bias)
+    early_set = (query_weight, key_weight, value_weight, gate_weight)
+    late_set = (output_weight, up_weight, down_weight, carry_weight)
+    low = jnp.bfloat16
+
+    def struct(*shape, dtype=low):
+        return jax.ShapeDtypeStruct(shape, dtype)
 
     def take(source, start, piece):
         rows = piece.shape[0]
@@ -287,43 +590,127 @@
             source[:, start + part * rows : start + (part + 1) * rows].reshape(devices * rows, width)
             for part in range(parts)
         ]
-        return (jnp.concatenate(blocks, axis=1) if parts > 1 else blocks[0]), start + parts * rows
-
-    place = 0
-    full_query, place = take(early_rows, place, query_weight)
-    full_key, place = take(early_rows, place, key_weight)
-    full_value, place = take(early_rows, place, value_weight)
-    full_gate, place = take(early_rows, place, gate_weight)
-    vector_rows = early_rows[:, place : place + -(-sum(v.shape[0] for v in vectors) // width)].reshape(devices, -1)
-    full_vectors = []
-    start = 0
-    for vector in vectors:
-        piece = vector_rows[:, start : start + vector.shape[0]].reshape(-1)
-        full_vectors.append(piece.astype(jnp.float32))
-        start += vector.shape[0]
-    gate_b, up_b, down_b, carry_b, gain_one, shift_one, gain_two, shift_two = full_vectors
-    place = 0
-    full_output, place = take(late_rows, place, output_weight)
-    full_up, place = take(late_rows, place, up_weight)
-    full_down, place = take(late_rows, place, down_weight)
-    full_carry, place = take(late_rows, place, carry_weight)
+        return joined(blocks, 1), start + parts * rows
+
+    def flat_rows(pieces):
+        return [piece[:, start : start + width] for piece in pieces for start in range(0, piece.shape[1], width)]
+
+    if direct:
+        early_count = 4 * rows_each + VECTOR_ROWS
+        late_count = sum(piece.shape[0] * piece.shape[1] // width for piece in late_set)
+        early, late = local_call(
+            pack_kernel,
+            2,
+            (struct(early_count, width), struct(late_count, width)),
+            jnp.full((devices,), device, jnp.int32),
+            early_set + late_set + tuple(vector.reshape(1, -1) for vector in vectors),
+        )
+        late_line = [late]
+        early_one = axis_z.rotate(early, 1)
+        z_one = axis_z.rotate(inputs, 1)
+        x_zero = axis_x.rotate(inputs, 1)
+        late_line.append(axis_z.rotate(late, 1))
+        early_two = axis_z.rotate(early_one, 1)
+        early_two, z_one, x_zero, late_line[1] = lax.optimization_barrier((early_two, z_one, x_zero, late_line[1]))
+        early_three = axis_z.rotate(early_two, 1)
+        z_two = axis_z.rotate(z_one, 1)
+        x_one = axis_x.rotate(z_one, 1)
+        late_line.append(axis_z.rotate(late_line[1], 1))
+        early_line = jnp.stack([early, early_one, early_two, early_three])
+        early_other = axis_x.rotate(early_line, 1)
+        early_other, z_two, x_one, late_line[2] = lax.optimization_barrier((early_other, z_two, x_one, late_line[2]))
+        early_plane = jnp.stack([early_line, early_other])
+        early_other = axis_y.rotate(early_plane, 1)
+        z_three = axis_z.rotate(z_two, 1)
+        x_two = axis_x.rotate(z_two, 1)
+        late_line.append(axis_z.rotate(late_line[2], 1))
+        early_all = jnp.stack([early_plane, early_other]).reshape(devices // 2, early_count, width)
+        early_other = axis_core.rotate(early_all, 1)
+        early_other, z_three, x_two, late_line[3] = lax.optimization_barrier(
+            (early_other, z_three, x_two, late_line[3])
+        )
+        x_three = axis_x.rotate(z_three, 1)
+        late_half = late_count // 2
+        late_x = jnp.stack([rows[:late_half] for rows in late_line])
+        late_y = jnp.stack([rows[late_half:] for rows in late_line])
+        late_x_other = axis_x.rotate(late_x, 1)
+        late_y_other = axis_y.rotate(late_y, 1)
+        x_three, late_x_other, late_y_other = lax.optimization_barrier((x_three, late_x_other, late_y_other))
+        late_x = jnp.stack([late_x, late_x_other])
+        late_y = jnp.stack([late_y, late_y_other])
+        late_x = jnp.stack([late_x, axis_y.rotate(late_x, 1)]).reshape(devices // 2, late_half, width)
+        late_y = jnp.stack([late_y, axis_x.rotate(late_y, 1)]).reshape(devices // 2, late_half, width)
+        late_x_other = axis_core.rotate(late_x, 1)
+        late_y_other = axis_core.rotate(late_y, 1)
+        other_places = jnp.transpose(places.reshape(2, 2, 2, 4), (0, 2, 1, 3)).reshape(-1)
+        full_output, full_up, full_down, full_carry = local_call(
+            unpack_late_kernel,
+            5,
+            (struct(width, width), struct(width, up_weight.shape[1]), struct(up_weight.shape[1], width), struct(width, width)),
+            jnp.stack([places, other_places]),
+            (late_x, late_x_other, late_y, late_y_other),
+        )
+        input_pieces = [[inputs, x_zero], [z_one, x_one], [z_two, x_two], [z_three, x_three]]
+        square = struct(width, width)
+        full_query, full_key, full_value, full_gate, vector_rows = local_call(
+            unpack_kernel,
+            3,
+            (square, square, square, square, struct(VECTOR_ROWS, width, dtype=jnp.float32)),
+            places,
+            (early_all, early_other),
+        )
+    else:
+        early_rows = lax.all_gather(jnp.concatenate(early_set), BOTH)
+        late_rows = lax.all_gather(jnp.concatenate(flat_rows(late_set)), BOTH)
+        place = 0
+        full_query, place = take(early_rows, place, query_weight)
+        full_key, place = take(early_rows, place, key_weight)
+        full_value, place = take(early_rows, place, value_weight)
+        full_gate, place = take(early_rows, place, gate_weight)
+        place = 0
+        full_output, place = take(late_rows, place, output_weight)
+        full_up, place = take(late_rows, place, up_weight)
+        full_down, place = take(late_rows, place, down_weight)
+        full_carry, place = take(late_rows, place, carry_weight)
+        lines = [lax.all_gather(vector, BOTH, tiled=True).reshape(-1, width) for vector in vectors]
+        lines = jnp.concatenate(lines).astype(jnp.float32)
+        vector_rows = jnp.pad(lines, ((0, VECTOR_ROWS - lines.shape[0]), (0, 0)))
+        input_pieces = []
+        along_z = inputs
+        for step_z in range(axis_z.size):
+            along_x = along_z
+            row = []
+            for step_x in range(axis_x.size):
+                row.append(along_x)
+                along_x = axis_x.rotate(along_x, 1) if step_x + 1 < axis_x.size else None
+            input_pieces.append(row)
+            along_z = axis_z.rotate(along_z, 1) if step_z + 1 < axis_z.size else None
+
+    carried = None
+    for step, row in enumerate(input_pieces):
+        carried = project(row, vector_rows, full_key, full_value, group_blocks * BLK, step, carried)
+    normed_group, key_group, value_group = carried
+    normed_low = normed_group[: inputs.shape[0]]
+
+    gate_b, down_b, carry_b, gain_one, shift_one, gain_two, shift_two = [vector_rows[line] for line in range(UP_B)]
+    up_b = vector_rows[UP_B : UP_B + up_weight.shape[1] // width].reshape(-1)
 
     own_start = lax.axis_index("seq") * block_count
     own_segments = lax.dynamic_slice_in_dim(block_segment, own_start, block_count)
     ancestor_slot, usable = ancestor_slots(block_segment, segment_parent, own_segments)
+    owner = ancestor_slot // block_count
+    away_z = (axis_z.position() - owner // axis_x.size) % axis_z.size
+    away_x = (axis_x.position() - owner % axis_x.size) % axis_x.size
+    relative_slot = (away_z * axis_x.size + away_x) * block_count + ancestor_slot % block_count
     slots = jnp.concatenate(
-        [ancestor_slot, jnp.sum(usable, axis=-1, keepdims=True, dtype=jnp.int32)], axis=-1
+        [relative_slot, jnp.sum(usable, axis=-1, keepdims=True, dtype=jnp.int32)], axis=-1
     )
 
     values_in = inputs.astype(jnp.float32)
-    normed_low = normalize(values_in, gain_one, shift_one).astype(jnp.bfloat16)
     query_low = (matmul(normed_low, full_query).astype(jnp.bfloat16) * (HD ** (-0.5))).astype(jnp.bfloat16)
     gate_open = jax.nn.sigmoid(matmul(normed_low, full_gate) + gate_b)
-    normed_group = normalize(input_group.astype(jnp.float32), gain_one, shift_one).astype(jnp.bfloat16)
-    key_group = matmul(normed_group, full_key).astype(jnp.bfloat16)
-    value_group = matmul(normed_group, full_value).astype(jnp.bfloat16)
-
-    cuts = max(1, group_blocks // 40)
+
+    cuts = min(4, max(1, group_blocks // 40) ** 2)
     heads = [slice(cut * width // cuts, (cut + 1) * width // cuts) for cut in range(cuts)]
     forward = [
         attend(slots, query_low[:, cols], key_group[:, cols], value_group[:, cols]) for cols in heads
@@ -343,43 +730,50 @@
     grad_out = cotangent.astype(jnp.float32)
     update_grad = (carry_open * grad_out).astype(jnp.bfloat16)
     carry_pre_grad = (grad_out * update * carry_open * (1.0 - carry_open)).astype(jnp.bfloat16)
-    grad_down = inner_rows(hidden_low, update_grad)
     grad_down_bias = column_sums(update_grad)
-    grad_carry = inner_rows(normed_second, carry_pre_grad)
     grad_carry_bias = column_sums(carry_pre_grad)
     silu_slope = up_sigmoid * (1.0 + up_pre * (1.0 - up_sigmoid))
     up_pre_grad = (against(update_grad, full_down) * silu_slope).astype(jnp.bfloat16)
-    grad_up = inner_rows(normed_second, up_pre_grad)
     grad_up_bias = column_sums(up_pre_grad)
     second_norm_grad = against(up_pre_grad, full_up) + against(carry_pre_grad, full_carry)
     second_pull = jax.vjp(normalize, middle, gain_two, shift_two)[1]
     middle_part, grad_second_gain, grad_second_shift = second_pull(second_norm_grad)
     middle_grad = grad_out + middle_part
 
-    def spread(grad, piece):
-        rows = piece.shape[0]
-        return [
-            grad[:, start : start + width].astype(jnp.bfloat16).reshape(devices, rows, width)
-            for start in range(0, grad.shape[1], width)
-        ]
-
-    def own(summed, start, piece):
-        rows = piece.shape[0]
-        parts = piece.shape[1] // width
-        blocks = [summed[start + part * rows : start + (part + 1) * rows] for part in range(parts)]
-        return (jnp.concatenate(blocks, axis=1) if parts > 1 else blocks[0]), start + parts * rows
-
-    first_pack = jnp.concatenate(
-        spread(grad_up, up_weight) + spread(grad_down, down_weight) + spread(grad_carry, carry_weight), axis=1
-    )
-    first_sum = lax.psum_scatter(first_pack, BOTH, scatter_dimension=0, tiled=True)[0].astype(jnp.float32)
-
     branch_grad = (gate_open * middle_grad).astype(jnp.bfloat16)
     gate_pre_grad = (middle_grad * branch * gate_open * (1.0 - gate_open)).astype(jnp.bfloat16)
-    grad_output = inner_rows(attended_low, branch_grad)
-    grad_gate = inner_rows(normed_low, gate_pre_grad)
     grad_gate_bias = column_sums(gate_pre_grad)
     attended_grad = against(branch_grad, full_output).astype(jnp.bfloat16)
+    if direct:
+        first_rows = late_count + rows_each
+        half = struct(devices // 2, first_rows, width)
+        first_keep, first_send = local_call(
+            first_grads_kernel,
+            9,
+            (half, half),
+            places,
+            (
+                hidden_low,
+                update_grad,
+                normed_second,
+                up_pre_grad,
+                carry_pre_grad,
+                attended_low,
+                branch_grad,
+                normed_low,
+                gate_pre_grad,
+            ),
+            (
+                pltpu.VMEM((up_weight.shape[1] // width, width, width), jnp.float32),
+                pltpu.VMEM((up_weight.shape[1], width), jnp.float32),
+                pltpu.VMEM((3, width, width), jnp.float32),
+            ),
+        )
+        near = (2, 2, 4, first_rows, width)
+        first_entry = pair_scatter(first_keep.reshape(near), first_send.reshape(near), axis_core)
+        first_keep, first_send = first_entry(0), first_entry(1)
+        attended_grad, first_keep, first_send = lax.optimization_barrier((attended_grad, first_keep, first_send))
+        first_y = pair_scatter(first_keep, first_send, axis_y)
 
     backward = [
         attend_backward(
@@ -390,73 +784,137 @@
             logsum,
             attended_low[:, cols],
             attended_grad[:, cols],
+            normed_group,
+            jnp.concatenate([full_key[:, cols], full_value[:, cols]], axis=1),
         )
         for cols, (mixed, logsum) in zip(heads, forward)
     ]
-    query_rows_grad = joined([query_part for query_part, sums in backward], 1)
+    query_rows_grad = joined([parts[0] for parts in backward], 1)
     part = width // cuts
-    sums = backward[0][1]
-    if cuts > 1:
-        sums = jnp.concatenate([sums[:part] for _, sums in backward] + [sums[part:] for _, sums in backward])
-
-    both_weight = jnp.concatenate([full_key, full_value], axis=1)
-    shared_grad = lax.dot_general(
-        sums, both_weight, (((0,), (1,)), ((), ())), preferred_element_type=jnp.float32
-    ).astype(jnp.bfloat16)
-    shared_sum = lax.psum_scatter(shared_grad, "seq", scatter_dimension=0, tiled=True).astype(jnp.float32)
-    grad_both = matmul(sums, normed_group)
-    grad_key = jnp.transpose(grad_both[:width])
-    grad_value = jnp.transpose(grad_both[width:])
-    grad_query = inner_rows(normed_low, query_rows_grad)
-    first_norm_grad = (
-        against(query_rows_grad, full_query) + shared_sum + against(gate_pre_grad, full_gate)
-    )
-    first_pull = jax.vjp(normalize, values_in, gain_one, shift_one)[1]
-    input_part, grad_first_gain, grad_first_shift = first_pull(first_norm_grad)
-    input_grad = middle_grad + input_part
-
-    vector_grads = (
+    both_grads, lanes = [
+        joined([parts[index][:part] for parts in backward] + [parts[index][part:] for parts in backward], 0)
+        if cuts > 1
+        else backward[0][index]
+        for index in (1, 2)
+    ]
+
+    shared_parts = [functools.reduce(add_low, pieces) for pieces in zip(*[parts[3:] for parts in backward])]
+
+    def over_x(step_z):
+        return ring_scatter(lambda step_x: shared_parts[step_z * axis_x.size + step_x], axis_x)
+
+    shared_sum = jnp.transpose(ring_scatter(over_x, axis_z).astype(jnp.float32))
+
+    zero_line = jnp.zeros((width,), jnp.float32)
+    local_lines = (
         grad_gate_bias,
-        grad_up_bias,
         grad_down_bias,
         grad_carry_bias,
-        grad_first_gain,
-        grad_first_shift,
+        zero_line,
+        zero_line,
         grad_second_gain,
         grad_second_shift,
+        grad_up_bias,
     )
-    vector_pack = jnp.concatenate([grad.reshape(devices, -1) for grad in vector_grads], axis=1)
-    count = -(-vector_pack.shape[1] // width)
-    vector_pack = jnp.pad(vector_pack, ((0, 0), (0, count * width - vector_pack.shape[1])))
-    second_pack = (
-        spread(grad_query, query_weight)
-        + spread(grad_key, key_weight)
-        + spread(grad_value, value_weight)
-        + spread(grad_output, output_weight)
-        + spread(grad_gate, gate_weight)
-        + [vector_pack.astype(jnp.bfloat16).reshape(devices, count, width)]
+    block = jnp.concatenate([line.reshape(-1, width) for line in local_lines])
+    block = jnp.pad(block, ((0, VECTOR_ROWS - block.shape[0]), (0, 0)))
+    if direct:
+        second_rows = 3 * rows_each + VECTOR_ROWS
+        half = struct(devices // 2, second_rows, width)
+        second_keep, second_send = local_call(
+            second_grads_kernel,
+            6,
+            (half, half),
+            places,
+            (
+                both_grads,
+                normed_low,
+                query_rows_grad,
+                gate_pre_grad,
+                lanes,
+                full_query,
+                full_key,
+                full_value,
+                full_gate,
+                vector_rows,
+                block,
+            ),
+            (pltpu.VMEM((3, width, width), jnp.float32),),
+        )
+        near = (2, 2, 4, second_rows, width)
+        second_entry = pair_scatter(second_keep.reshape(near), second_send.reshape(near), axis_core)
+        second_y = pair_scatter(second_entry(0), second_entry(1), axis_y)
+
+        def far(y_entry):
+            along = [y_entry(index) for index in range(2)]
+            over_z = ring_scatter(lambda back: jnp.stack([along[0][back], along[1][back]]), axis_z)
+            return ring_scatter(lambda back: over_z[back], axis_x)
+
+        weight_sum = jnp.concatenate([far(first_y), far(second_y)]).astype(jnp.float32)
+    else:
+        grad_key = jnp.transpose(both_grads[:width])
+        grad_value = jnp.transpose(both_grads[width:])
+        grad_query = inner_rows(normed_low, query_rows_grad)
+        grad_gate = inner_rows(normed_low, gate_pre_grad)
+        both_sums = jnp.sum(lanes, axis=1)
+        weights = [weight.astype(jnp.float32) for weight in (full_query, full_key, full_value, full_gate)]
+        line_sums = (column_sums(query_rows_grad), both_sums[:width], both_sums[width:], grad_gate_bias)
+        shift_line = sum(jnp.sum(weight * line, axis=1) for weight, line in zip(weights, line_sums))
+        weighted = sum(
+            jnp.sum(weight * grad, axis=1)
+            for weight, grad in zip(weights, (grad_query, grad_key, grad_value, grad_gate))
+        )
+        block = block.at[GAIN_ONE].set((weighted - shift_one * shift_line) / gain_one).at[SHIFT_ONE].set(shift_line)
+        grads = (
+            (inner_rows(normed_second, up_pre_grad), up_weight),
+            (inner_rows(hidden_low, update_grad), down_weight),
+            (inner_rows(normed_second, carry_pre_grad), carry_weight),
+            (inner_rows(attended_low, branch_grad), output_weight),
+            (grad_gate, gate_weight),
+            (grad_query, query_weight),
+            (grad_key, key_weight),
+            (grad_value, value_weight),
+        )
+        pack = [
+            cut.astype(low).reshape(devices, piece.shape[0], width)
+            for grad, piece in grads
+            for cut in flat_rows((grad,))
+        ]
+        pack.append(jnp.broadcast_to(block.astype(low), (devices, VECTOR_ROWS, width)))
+        pack = jnp.concatenate(pack, axis=1)
+        pack = jnp.pad(pack, ((0, 0), (0, -pack.shape[1] % 16), (0, 0)))
+        weight_sum = lax.psum_scatter(pack, BOTH, scatter_dimension=0, tiled=True)[0].astype(jnp.float32)
+
+    def own(start, piece):
+        rows = piece.shape[0]
+        parts = piece.shape[1] // width
+        blocks = [weight_sum[start + part * rows : start + (part + 1) * rows] for part in range(parts)]
+        return joined(blocks, 1), start + parts * rows
+
+    local_grad = against(query_rows_grad, full_query) + against(gate_pre_grad, full_gate)
+    centered = values_in - jnp.mean(values_in, axis=-1, keepdims=True)
+    scale = lax.rsqrt(jnp.mean(centered * centered, axis=-1, keepdims=True) + EPSILON)
+    hat = centered * scale
+    pull = (local_grad + shared_sum) * gain_one
+    input_grad = middle_grad + scale * (
+        pull - jnp.mean(pull, axis=-1, keepdims=True) - hat * jnp.mean(pull * hat, axis=-1, keepdims=True)
     )
-    second_pack = jnp.concatenate(second_pack, axis=1)
-    second_pack = jnp.pad(second_pack, ((0, 0), (0, -second_pack.shape[1] % 16), (0, 0)))
-    second_sum = lax.psum_scatter(second_pack, BOTH, scatter_dimension=0, tiled=True)[0].astype(jnp.float32)
 
     place = 0
-    own_up, place = own(first_sum, place, up_weight)
-    own_down, place = own(first_sum, place, down_weight)
-    own_carry, place = own(first_sum, place, carry_weight)
-    place = 0
-    own_query, place = own(second_sum, place, query_weight)
-    own_key, place = own(second_sum, place, key_weight)
-    own_value, place = own(second_sum, place, value_weight)
-    own_output, place = own(second_sum, place, output_weight)
-    own_gate, place = own(second_sum, place, gate_weight)
-    own_vectors = second_sum[place : place + count].reshape(-1)
+    own_up, place = own(place, up_weight)
+    own_down, place = own(place, down_weight)
+    own_carry, place = own(place, carry_weight)
+    own_output, place = own(place, output_weight)
+    own_gate, place = own(place, gate_weight)
+    own_query, place = own(place, query_weight)
+    own_key, place = own(place, key_weight)
+    own_value, place = own(place, value_weight)
     vector_out = []
-    start = 0
-    for vector in vectors:
-        vector_out.append(own_vectors[start : start + vector.shape[0]])
-        start += vector.shape[0]
-    gate_bg, up_bg, down_bg, carry_bg, gain_one_g, shift_one_g, gain_two_g, shift_two_g = vector_out
+    for index, vector in enumerate(vectors):
+        count = vector.shape[0]
+        lines = weight_sum[place + index : place + index + count * devices // width].reshape(-1)
+        vector_out.append(lax.dynamic_slice_in_dim(lines, device * count, count))
+    gate_bg, down_bg, carry_bg, gain_one_g, shift_one_g, gain_two_g, shift_two_g, up_bg = vector_out
     return (
         output,
         input_grad,

time: 632 us -> 380 us (0.60); the launches traced: 620 us -> 376 us
  waiting for transfers between devices: 423 us -> 136 us
  Pallas kernels: 48.6 us -> 106 us
  starting transfers between devices: 0.5 us -> 38.1 us
  matrix products: 61.9 us -> 24.9 us
  local copies, waits for them, and re-layouts: 51.6 us -> 36.2 us
  other arithmetic: 19.3 us -> 32.8 us
  between operations: 15.1 us -> 1.96 us
    reduce_scatter x2 -> x0, waiting for transfers between devices: 200 us -> none  [the longest x1 101 us: shards(): lax.psum_scatter(first_pack, BOTH, scatter_dimension=0, tiled=True)[0]]
    all_gather x3 -> x0, waiting for transfers between devices: 157 us -> none  [the longest x1 80.6 us: shards(): input_group = lax.all_gather(inputs, 'seq', axis=0, tiled=True)]
    ppermute x0 -> x41, waiting for transfers between devices: none -> 136 us  [rotate(): return lax.ppermute(values, self.name, pairs)]
    unnamed x7 -> x0, waiting for transfers between devices: 66.1 us -> none
    pallas_call x2 -> x11, Pallas kernels: 48.6 us -> 106 us  [the longest x1 39.7 us: attend_backward(): pl.pallas_call(backward_kernel, cost_estimate=about(40), out_shape=(jax.S...]
    ppermute x0 -> x41, starting transfers between devices: none -> 38.1 us  [rotate(): return lax.ppermute(values, self.name, pairs)]
    dot_general x9 -> x6, matrix products: 32.6 us -> 12.3 us  [matmul(): return jnp.dot(left_side, right_side, preferred_element_type=jnp.float32)]
    dot_general x7 -> x0, matrix products: 19.4 us -> none  [the longest x1 10.2 us: shards(): lax.dot_general(sums, both_weight, (((0,), (1,)), ((), ())), preferred_el...]
  transfers between devices with their start and end apart: 6 -> 41, of which waited for: 6 -> 16; matrix products, arithmetic and copies ran while one was open for 14% -> 15% of each run, Pallas kernels for 3% -> 12%
where the time goes in v2:
time: 380 us; the launch traced here: 376 us
  waiting for transfers between devices  136 us (36%)
  Pallas kernels  106 us (28%)
  starting transfers between devices  38.1 us (10%)
  local copies, waits for them, and re-layouts  36.2 us (10%)
  other arithmetic  32.8 us (9%)
  matrix products  24.9 us (7%)
    ppermute x41, waiting for transfers between devices, rotate(): return lax.ppermute(values, self.name, pairs)  136 us
    pallas_call x1, Pallas kernels, attend_backward(): pl.pallas_call(backward_kernel, cost_estimate=about(40), out_shape=(jax.S...  39.7 us
    ppermute x41, starting transfers between devices, rotate(): return lax.ppermute(values, self.name, pairs)  38.1 us
    pallas_call x5, Pallas kernels, local_call(): pl.pallas_call(kernel, cost_estimate=about(cost), out_shape=outs, in_spec...  28.1 us
    pallas_call x4, Pallas kernels, project(): pl.pallas_call(body, cost_estimate=about(4), grid=(1,), out_shape=(whole,...  19.5 us
    pallas_call x1, Pallas kernels, attend(): pl.pallas_call(forward_kernel, cost_estimate=about(18), out_shape=(jax.Sh...  18.9 us
    pallas_call x8, local copies, waits for them, and re-layouts, attend_backward(): pl.pallas_call(backward_kernel, cost_estimate=about(40), out_shape=(jax.S...  15.4 us
    dot_general x6, matrix products, against(): lax.dot_general(left_side, right_side, (((1,), (1,)), ((), ())), preferre...  12.6 us
  transfers between devices with their start and end apart: 41, of which 16 were waited for; matrix products, arithmetic and copies ran while one was open for 15% of the time, Pallas kernels for 12%

profile of v2, /device:TPU:28, one launch (start us, length us, event | category | flops | bytes accessed | tf_op | source)
XLA Modules:
  0.0 376.3 jit_solution(587740685512910057)
XLA Ops:
  11.0 9.3 %collective-permute-done = bf16[80,512]{1,0:T(8,128)(2,1)S(1)} collective-permute-done((bf16[80,512]{1,0:T(8,128)(2,1)}, bf16[80,512]{1,0:T(8,128)(2,1)S(1)}, u32[]{:S(2)}, u32[]{:S(2)}) %collective-permute-start) | collective-permute-done | bytes 81952 | tf_op jit(solution)/shard_map/ppermute | solution.py:321
  20.3 2.0 collective-permute-start.1
  22.5 2.2 collective-permute-done.1
  24.8 3.9 %collective-permute-start.7 = (bf16[640,512]{1,0:T(8,128)(2,1)S(1)}, bf16[640,512]{1,0:T(8,128)(2,1)S(1)}, u32[]{:S(2)}, u32[]{:S(2)}) collective-permute-start(bf16[640,512]{1,0:T(8,128)(2,1)S(1)} %collective-permute-done.2.refs_0_), channel_id=1, source_target_pairs={{0,2},{1,3},{2,4},{3,5},{4,6},{5,7},{6,0},{7,1},{8,10},{9,11},{10,... | collective-permute-start | bytes 1966088 | tf_op jit(solution)/shard_map/ppermute | solution.py:321
  30.4 11.4 %collective-permute-done.5 = bf16[80,512]{1,0:T(8,128)(2,1)S(1)} collective-permute-done((bf16[80,512]{1,0:T(8,128)(2,1)S(1)}, bf16[80,512]{1,0:T(8,128)(2,1)S(1)}, u32[]{:S(2)}, u32[]{:S(2)}) %collective-permute-start.5) | collective-permute-done | bytes 81952 | tf_op jit(solution)/shard_map/ppermute | solution.py:321
  44.3 3.9 %collective-permute-start.9 = (bf16[160,512]{1,0:T(8,128)(2,1)S(1)}, bf16[160,512]{1,0:T(8,128)(2,1)S(1)}, u32[]{:S(2)}, u32[]{:S(2)}) collective-permute-start(bf16[160,512]{1,0:T(8,128)(2,1)S(1)} %collective-permute-done.4), channel_id=1, source_target_pairs={{0,2},{1,3},{2,4},{3,5},{4,6},{5,7},{6,0},{7,1},{8,10},{9,11},{10,... | collective-permute-start | bytes 491528 | tf_op jit(solution)/shard_map/ppermute | solution.py:321
  48.8 2.3 collective-permute-done.9
  54.5 11.1 %collective-permute-done.10 = bf16[2,4,80,512]{3,2,1,0:T(8,128)(2,1)S(1)} collective-permute-done((bf16[2,4,80,512]{3,2,1,0:T(8,128)(2,1)}, bf16[2,4,80,512]{3,2,1,0:T(8,128)(2,1)S(1)}, u32[]{:S(2)}, u32[]{:S(2)}) %collective-permute-start.10) | collective-permute-done | bytes 655392 | tf_op jit(solution)/shard_map/ppermute | solution.py:321
  70.0 3.0 collective-permute-start.12
  75.5 15.7 %collective-permute-done.14 = bf16[160,512]{1,0:T(8,128)(2,1)S(1)} collective-permute-done((bf16[160,512]{1,0:T(8,128)(2,1)}, bf16[160,512]{1,0:T(8,128)(2,1)S(1)}, u32[]{:S(2)}, u32[]{:S(2)}) %collective-permute-start.14) | collective-permute-done | bytes 163872 | tf_op jit(solution)/shard_map/ppermute | solution.py:321
  94.8 3.2 shard_map.332
  98.0 4.8 %shard_map.333 = (bf16[5120,512]{1,0:T(8,128)(2,1)}, bf16[5120,512]{1,0:T(8,128)(2,1)}, bf16[5120,512]{1,0:T(8,128)(2,1)}) custom-call(bf16[640,512]{1,0:T(8,128)(2,1)} %refs_0_.3, bf16[640,512]{1,0:T(8,128)(2,1)} %collective-permute-done.3.refs_1_, f32[16,512]{1,0:T(8,128)} %get-tuple-element.88.refs_2_.vectors_ref, ...), custom_call_target="tpu_custom_call" | custom-call | flops 4000000000 | bytes 4000000 | tf_op jit(solution)/shard_map/pallas_call | solution.py:294
  102.8 4.9 %shard_map.334 = (bf16[5120,512]{1,0:T(8,128)(2,1)}, bf16[5120,512]{1,0:T(8,128)(2,1)}, bf16[5120,512]{1,0:T(8,128)(2,1)}) custom-call(bf16[640,512]{1,0:T(8,128)(2,1)} %copy-done.17, bf16[640,512]{1,0:T(8,128)(2,1)} %copy-done.20, f32[16,512]{1,0:T(8,128)} %get-tuple-element.88.refs_2_.vectors_ref, ...), custom_call_target="tpu_custom_call", output_to_operand_aliasing={{0}: (5, {}), {1}: (6, {}), {2}: (7, {})} | custom-call | flops 4000000000 | bytes 4000000 | tf_op jit(solution)/shard_map/pallas_call | solution.py:294
  108.3 4.9 %shard_map.335 = (bf16[5120,512]{1,0:T(8,128)(2,1)}, bf16[5120,512]{1,0:T(8,128)(2,1)}, bf16[5120,512]{1,0:T(8,128)(2,1)}) custom-call(bf16[640,512]{1,0:T(8,128)(2,1)} %copy-done.18, bf16[640,512]{1,0:T(8,128)(2,1)} %copy-done.23, f32[16,512]{1,0:T(8,128)} %get-tuple-element.88.refs_2_.vectors_ref, ...), custom_call_target="tpu_custom_call", output_to_operand_aliasing={{0}: (5, {}), {1}: (6, {}), {2}: (7, {})} | custom-call | flops 4000000000 | bytes 4000000 | tf_op jit(solution)/shard_map/pallas_call | solution.py:294
  118.2 4.8 %shard_map.336 = (bf16[5120,512]{1,0:T(8,128)(2,1)}, bf16[5120,512]{1,0:T(8,128)(2,1)}, bf16[5120,512]{1,0:T(8,128)(2,1)}) custom-call(bf16[640,512]{1,0:T(8,128)(2,1)} %copy-done.21, bf16[640,512]{1,0:T(8,128)(2,1)} %copy-done.22, f32[16,512]{1,0:T(8,128)} %get-tuple-element.88.refs_2_.vectors_ref, ...), custom_call_target="tpu_custom_call", output_to_operand_aliasing={{0}: (5, {}), {1}: (6, {}), {2}: (7, {})} | custom-call | flops 4000000000 | bytes 4000000 | tf_op jit(solution)/shard_map/pallas_call | solution.py:294
  123.0 2.0 slice.273.normed_ref
  125.0 2.4 fusion.24.query_ref
  127.5 3.8 collective-permute-done.18
  136.0 18.9 %shard_map.337 = (bf16[640,512]{1,0:T(8,128)(2,1)}, f32[640,128]{1,0:T(8,128)}) custom-call(s32[5,11]{1,0:T(8,128)} %pad_add_fusion.slots_ref, bf16[640,512]{1,0:T(8,128)(2,1)} %fusion.24.query_ref, bf16[5120,512]{1,0:T(8,128)(2,1)} %get-tuple-element.106.key_ref.key_source, bf16[5120,512]{1,0:T(8,128)(2,1)} %get-tuple-element.107.value_ref.value_source), custom_call_target="tpu_custom_call" | custom-call | flops 17999998976 | bytes 18000000 | tf_op jit(solution)/shard_map/pallas_call | solution.py:222
  155.0 5.3 %shard_map.338 = (bf16[512,512]{1,0:T(8,128)(2,1)}, bf16[512,2048]{1,0:T(8,128)(2,1)}, bf16[2048,512]{1,0:T(8,128)(2,1)}, bf16[512,512]{1,0:T(8,128)(2,1)}) custom-call(s32[2,32]{1,0:T(2,128)} %pad_add_fusion.1.place_ref, bf16[16,80,512]{2,1,0:T(8,128)(2,1)} %bitcast.203, bf16[16,80,512]{2,1,0:T(8,128)(2,1)} %collective-permute-done.19.line_other_ref, ...), custom_call_target="tpu_custom_call" | custom-call | flops 5000000000 | bytes 5000000 | tf_op jit(solution)/shard_map/pallas_call | solution.py:530
  161.9 2.0 fusion.85
  165.6 2.1 multiply_convert_fusion.1
  169.8 2.6 convert_reduce_fusion.3
  173.8 3.5 convert_reduce_fusion
  177.2 2.5 multiply_reduce_fusion
  181.9 11.1 %shard_map.339 = (bf16[16,176,512]{2,1,0:T(8,128)(2,1)}, bf16[16,176,512]{2,1,0:T(8,128)(2,1)}) custom-call(s32[32]{0:T(128)} %fusion.46.place_ref, bf16[640,2048]{1,0:T(8,128)(2,1)} %copy-done.44, bf16[640,512]{1,0:T(8,128)(2,1)} %copy-done.46, bf16[640,512]{1,0:T(8,128)(2,1)} %copy-done.31, bf16[640,2048]{1,0:T(8,128)(2,1)} %copy-done.42, ...), custom_call_target="tpu_custom_call" | custom-call | flops 8999999488 | bytes 9000000 | tf_op jit(solution)/shard_map/pallas_call | solution.py:530
  196.7 2.5 convolution_convert_fusion.mixed_grad_ref
  199.2 2.0 fusion.87
  201.2 4.3 %fusion = (bf16[2,4,176,512]{3,2,1,0:T(8,128)(2,1)}, bf16[2,4,176,512]{3,2,1,0:T(8,128)(2,1)}) fusion(bf16[2,4,176,512]{3,2,1,0:T(8,128)(2,1)S(1)} %bitcast.196, bf16[2,2,4,176,512]{4,3,2,1,0:T(8,128)(2,1)} %collective-permute-done.22, bf16[2,4,176,512]{3,2,1,0:T(8,128)(2,1)S(1)} %bitcast.197), kind=kLoop, calls=%fused_computation.5 | loop fusion | flops 5767168 | bytes 8650752 | tf_op jit(solution)/shard_map/convert_element_type | solution.py:350
  205.4 39.7 %shard_map.340 = (bf16[640,512]{1,0:T(8,128)(2,1)}, f32[1024,512]{1,0:T(8,128)}, f32[1024,128]{1,0:T(8,128)}, bf16[512,640]{1,0:T(8,128)(2,1)}, bf16[512,640]{1,...) custom-call(s32[5,11]{1,0:T(8,128)} %pad_add_fusion.slots_ref, ...), custom_call_target="tpu_custom_call" | custom-call | flops 40000000000 | bytes 40000000 | tf_op jit(solution)/shard_map/pallas_call | solution.py:246
  245.1 6.7 %shard_map.341 = (bf16[16,64,512]{2,1,0:T(8,128)(2,1)}, bf16[16,64,512]{2,1,0:T(8,128)(2,1)}) custom-call(s32[32]{0:T(128)} %fusion.46.place_ref, f32[1024,512]{1,0:T(8,128)} %get-tuple-element.130.both_grads_ref, bf16[640,512]{1,0:T(8,128)(2,1)} %slice.273.normed_ref, bf16[640,512]{1,0:T(8,128)(2,1)} %get-tuple-element.119.query_grad_ref, ...), custom_call_target="tpu_custom_call" | custom-call | flops 6000000000 | bytes 6000000 | tf_op jit(solution)/shard_map/pallas_call | solution.py:530
  259.8 2.2 copy.94
  262.0 2.2 copy.88
  264.2 2.2 copy.90
  266.4 2.2 copy.89
  270.1 2.2 copy.92
  272.2 2.2 copy.91
  274.4 1.9 convolution_add_fusion
  278.6 7.2 %collective-permute-done.23 = bf16[512,640]{0,1:T(8,128)(2,1)} collective-permute-done((bf16[512,640]{0,1:T(8,128)(2,1)}, bf16[512,640]{0,1:T(8,128)(2,1)}, u32[]{:S(2)}, u32[]{:S(2)}) %collective-permute-start.23) | collective-permute-done | bytes 655392 | tf_op jit(solution)/shard_map/ppermute | solution.py:321
  290.3 7.3 %collective-permute-done.36 = bf16[2,4,64,512]{3,2,1,0:T(8,128)(2,1)S(1)} collective-permute-done((bf16[2,4,64,512]{3,2,1,0:T(8,128)(2,1)S(1)}, bf16[2,4,64,512]{3,2,1,0:T(8,128)(2,1)S(1)}, u32[]{:S(2)}, u32[]{:S(2)}) %collective-permute-start.36) | collective-permute-done | bytes 524320 | tf_op jit(solution)/shard_map/ppermute | solution.py:321
  298.1 10.6 %collective-permute-done.37 = bf16[2,64,512]{2,1,0:T(8,128)(2,1)S(1)} collective-permute-done((bf16[2,64,512]{2,1,0:T(8,128)(2,1)S(1)}, bf16[2,64,512]{2,1,0:T(8,128)(2,1)S(1)}, u32[]{:S(2)}, u32[]{:S(2)}) %collective-permute-start.37) | collective-permute-done | bytes 131104 | tf_op jit(solution)/shard_map/ppermute | solution.py:321
  310.5 2.5 collective-permute-start.26
  313.1 11.6 %collective-permute-done.38 = bf16[2,64,512]{2,1,0:T(8,128)(2,1)S(1)} collective-permute-done((bf16[2,64,512]{2,1,0:T(8,128)(2,1)S(1)}, bf16[2,64,512]{2,1,0:T(8,128)(2,1)S(1)}, u32[]{:S(2)}, u32[]{:S(2)}) %collective-permute-start.38) | collective-permute-done | bytes 131104 | tf_op jit(solution)/shard_map/ppermute | solution.py:321
  324.9 16.6 %collective-permute-done.39 = bf16[2,64,512]{2,1,0:T(8,128)(2,1)S(1)} collective-permute-done((bf16[2,64,512]{2,1,0:T(8,128)(2,1)S(1)}, bf16[2,64,512]{2,1,0:T(8,128)(2,1)S(1)}, u32[]{:S(2)}, u32[]{:S(2)}) %collective-permute-start.39) | collective-permute-done | bytes 131104 | tf_op jit(solution)/shard_map/ppermute | solution.py:321
  342.1 3.7 collective-permute-done.32
  346.4 12.7 %collective-permute-done.33 = bf16[2,176,512]{2,1,0:T(8,128)(2,1)S(1)} collective-permute-done((bf16[2,176,512]{2,1,0:T(8,128)(2,1)S(1)}, bf16[2,176,512]{2,1,0:T(8,128)(2,1)S(1)}, u32[]{:S(2)}, u32[]{:S(2)}) %collective-permute-start.33) | collective-permute-done | bytes 360480 | tf_op jit(solution)/shard_map/ppermute | solution.py:321
  359.5 9.3 %collective-permute-done.28 = bf16[512,640]{0,1:T(8,128)(2,1)S(1)} collective-permute-done((bf16[512,640]{0,1:T(8,128)(2,1)S(1)}, bf16[512,640]{0,1:T(8,128)(2,1)S(1)}, u32[]{:S(2)}, u32[]{:S(2)}) %collective-permute-start.28) | collective-permute-done | bytes 655392 | tf_op jit(solution)/shard_map/ppermute | solution.py:321
  368.8 2.0 fusion.80
  (288 shorter events, 77.2 us)
Async XLA Ops:
  0.7 24.1 %collective-permute-start.2 = (bf16[640,512]{1,0:T(8,128)(2,1)}, bf16[640,512]{1,0:T(8,128)(2,1)S(1)}, u32[]{:S(2)}, u32[]{:S(2)}) collective-permute-start(bf16[640,512]{1,0:T(8,128)(2,1)} %refs_0_.3), channel_id=1, source_target_pairs={{0,2},{1,3},{2,4},{3,5},{4,6},{5,7},{6,0},{7,1},{8,10},{9,11},{10,... | collective-permute-start | bytes 1966088 | tf_op jit(solution)/shard_map/ppermute | solution.py:321
  0.9 23.8 %collective-permute-start.3 = (bf16[640,512]{1,0:T(8,128)(2,1)}, bf16[640,512]{1,0:T(8,128)(2,1)}, u32[]{:S(2)}, u32[]{:S(2)}) collective-permute-start(bf16[640,512]{1,0:T(8,128)(2,1)} %refs_0_.3), channel_id=1, source_target_pairs={{0,1},{1,0},{2,3},{3,2},{4,5},{5,4},{6,7},{7,6},{8,9},{9,8},{10,11... | collective-permute-start | bytes 1966088 | tf_op jit(solution)/shard_map/ppermute | solution.py:321
  4.8 15.5 %collective-permute-start = (bf16[80,512]{1,0:T(8,128)(2,1)}, bf16[80,512]{1,0:T(8,128)(2,1)S(1)}, u32[]{:S(2)}, u32[]{:S(2)}) collective-permute-start(bf16[80,512]{1,0:T(8,128)(2,1)} %get-tuple-element.76), channel_id=1, source_target_pairs={{0,2},{1,3},{2,4},{3,5},{4,6},{5,7},{6,0},{7,1},{8,10},{9,11},{10,... | collective-permute-start | bytes 245768 | tf_op jit(solution)/shard_map/ppermute | solution.py:321
  6.4 18.4 %collective-permute-start.4 = (bf16[160,512]{1,0:T(8,128)(2,1)}, bf16[160,512]{1,0:T(8,128)(2,1)S(1)}, u32[]{:S(2)}, u32[]{:S(2)}) collective-permute-start(bf16[160,512]{1,0:T(8,128)(2,1)} %get-tuple-element.77), channel_id=1, source_target_pairs={{0,2},{1,3},{2,4},{3,5},{4,6},{5,7},{6,0},{7,1},{8,10},{9,11},{10,... | collective-permute-start | bytes 491528 | tf_op jit(solution)/shard_map/ppermute | solution.py:321
  20.3 4.4 %collective-permute-start.1 = (bf16[80,512]{1,0:T(8,128)(2,1)S(1)}, bf16[80,512]{1,0:T(8,128)(2,1)S(1)}, u32[]{:S(2)}, u32[]{:S(2)}) collective-permute-start(bf16[80,512]{1,0:T(8,128)(2,1)S(1)} %collective-permute-done), channel_id=1, source_target_pairs={{0,2},{1,3},{2,4},{3,5},{4,6},{5,7},{6,0},{7,1},{8,10},{9,11},{10,... | collective-permute-start | bytes 245768 | tf_op jit(solution)/shard_map/ppermute | solution.py:321
  24.7 28.1 %copy-start.17 = (bf16[640,512]{1,0:T(8,128)(2,1)}, bf16[640,512]{1,0:T(8,128)(2,1)S(1)}, u32[]{:S(2)}) copy-start(bf16[640,512]{1,0:T(8,128)(2,1)S(1)} %collective-permute-done.2.refs_0_) | copy-start | bytes 1966084
  24.8 26.3 %collective-permute-start.7 = (bf16[640,512]{1,0:T(8,128)(2,1)S(1)}, bf16[640,512]{1,0:T(8,128)(2,1)S(1)}, u32[]{:S(2)}, u32[]{:S(2)}) collective-permute-start(bf16[640,512]{1,0:T(8,128)(2,1)S(1)} %collective-permute-done.2.refs_0_), channel_id=1, source_target_pairs={{0,2},{1,3},{2,4},{3,5},{4,6},{5,7},{6,0},{7,1},{8,10},{9,11},{10,... | collective-permute-start | bytes 1966088 | tf_op jit(solution)/shard_map/ppermute | solution.py:321
  28.6 22.5 %collective-permute-start.8 = (bf16[640,512]{1,0:T(8,128)(2,1)S(1)}, bf16[640,512]{1,0:T(8,128)(2,1)S(1)}, u32[]{:S(2)}, u32[]{:S(2)}) collective-permute-start(bf16[640,512]{1,0:T(8,128)(2,1)S(1)} %collective-permute-done.2.refs_0_), channel_id=1, source_target_pairs={{0,1},{1,0},{2,3},{3,2},{4,5},{5,4},{6,7},{7,6},{8,9},{9,8},{10,11... | collective-permute-start | bytes 1966088 | tf_op jit(solution)/shard_map/ppermute | solution.py:321
  30.2 11.7 %collective-permute-start.5 = (bf16[80,512]{1,0:T(8,128)(2,1)S(1)}, bf16[80,512]{1,0:T(8,128)(2,1)S(1)}, u32[]{:S(2)}, u32[]{:S(2)}) collective-permute-start(bf16[80,512]{1,0:T(8,128)(2,1)S(1)} %collective-permute-done.1), channel_id=1, source_target_pairs={{0,2},{1,3},{2,4},{3,5},{4,6},{5,7},{6,0},{7,1},{8,10},{9,11},{10,... | collective-permute-start | bytes 245768 | tf_op jit(solution)/shard_map/ppermute | solution.py:321
  42.8 8.3 %collective-permute-start.6 = (bf16[4,80,512]{2,1,0:T(8,128)(2,1)S(1)}, bf16[4,80,512]{2,1,0:T(8,128)(2,1)S(1)}, u32[]{:S(2)}, u32[]{:S(2)}) collective-permute-start(bf16[4,80,512]{2,1,0:T(8,128)(2,1)S(1)} %get-tuple-element.202), channel_id=1, source_target_pairs={{0,1},{1,0},{2,3},{3,2},{4,5},{5,4},{6,7},{7,6},{8,9},{9,8},{10,11... | collective-permute-start | bytes 983048 | tf_op jit(solution)/shard_map/ppermute | solution.py:321
  44.3 6.7 %collective-permute-start.9 = (bf16[160,512]{1,0:T(8,128)(2,1)S(1)}, bf16[160,512]{1,0:T(8,128)(2,1)S(1)}, u32[]{:S(2)}, u32[]{:S(2)}) collective-permute-start(bf16[160,512]{1,0:T(8,128)(2,1)S(1)} %collective-permute-done.4), channel_id=1, source_target_pairs={{0,2},{1,3},{2,4},{3,5},{4,6},{5,7},{6,0},{7,1},{8,10},{9,11},{10,... | collective-permute-start | bytes 491528 | tf_op jit(solution)/shard_map/ppermute | solution.py:321
  51.1 14.6 %copy-start.38 = (bf16[160,512]{1,0:T(8,128)(2,1)}, bf16[160,512]{1,0:T(8,128)(2,1)S(1)}, u32[]{:S(2)}) copy-start(bf16[160,512]{1,0:T(8,128)(2,1)S(1)} %collective-permute-done.9) | copy-start | bytes 491524
  52.9 12.7 %collective-permute-start.10 = (bf16[2,4,80,512]{3,2,1,0:T(8,128)(2,1)}, bf16[2,4,80,512]{3,2,1,0:T(8,128)(2,1)S(1)}, u32[]{:S(2)}, u32[]{:S(2)}) collective-permute-start(bf16[2,4,80,512]{3,2,1,0:T(8,128)(2,1)} %get-tuple-element.186), channel_id=1, source_target_pairs={{0,16},{8,24},{16,0},{24,8},{1,17},{9,25},{17,1},{25,9},{2,18},{10... | collective-permute-start | bytes 1966088 | tf_op jit(solution)/shard_map/ppermute | solution.py:321
  67.8 25.3 %copy-start.13 = (bf16[2,2,4,80,512]{4,3,2,1,0:T(8,128)(2,1)}, bf16[2,2,4,80,512]{4,3,2,1,0:T(8,128)(2,1)S(1)}, u32[]{:S(2)}) copy-start(bf16[2,2,4,80,512]{4,3,2,1,0:T(8,128)(2,1)S(1)} %pad_maximum_fusion) | copy-start | bytes 3932164
  67.8 23.4 %collective-permute-start.11 = (bf16[16,80,512]{2,1,0:T(8,128)(2,1)S(1)}, bf16[16,80,512]{2,1,0:T(8,128)(2,1)}, u32[]{:S(2)}, u32[]{:S(2)}) collective-permute-start(bf16[16,80,512]{2,1,0:T(8,128)(2,1)S(1)} %bitcast.200), channel_id=1, source_target_pairs={{0,8},{8,0},{16,24},{24,16},{1,9},{9,1},{17,25},{25,17},{2,10},{10... | collective-permute-start | bytes 3932168 | tf_op jit(solution)/shard_map/ppermute | solution.py:321
  70.0 21.2 %collective-permute-start.12 = (bf16[640,512]{1,0:T(8,128)(2,1)S(1)}, bf16[640,512]{1,0:T(8,128)(2,1)S(1)}, u32[]{:S(2)}, u32[]{:S(2)}) collective-permute-start(bf16[640,512]{1,0:T(8,128)(2,1)S(1)} %copy-done.19), channel_id=1, source_target_pairs={{0,2},{1,3},{2,4},{3,5},{4,6},{5,7},{6,0},{7,1},{8,10},{9,11},{10,... | collective-permute-start | bytes 1966088 | tf_op jit(solution)/shard_map/ppermute | solution.py:321
  73.0 18.2 %collective-permute-start.13 = (bf16[640,512]{1,0:T(8,128)(2,1)S(1)}, bf16[640,512]{1,0:T(8,128)(2,1)S(1)}, u32[]{:S(2)}, u32[]{:S(2)}) collective-permute-start(bf16[640,512]{1,0:T(8,128)(2,1)S(1)} %copy-done.19), channel_id=1, source_target_pairs={{0,1},{1,0},{2,3},{3,2},{4,5},{5,4},{6,7},{7,6},{8,9},{9,8},{10,11... | collective-permute-start | bytes 1966088 | tf_op jit(solution)/shard_map/ppermute | solution.py:321
  74.1 17.1 %collective-permute-start.14 = (bf16[160,512]{1,0:T(8,128)(2,1)}, bf16[160,512]{1,0:T(8,128)(2,1)S(1)}, u32[]{:S(2)}, u32[]{:S(2)}) collective-permute-start(bf16[160,512]{1,0:T(8,128)(2,1)} %copy-done.38), channel_id=1, source_target_pairs={{0,2},{1,3},{2,4},{3,5},{4,6},{5,7},{6,0},{7,1},{8,10},{9,11},{10,... | collective-permute-start | bytes 491528 | tf_op jit(solution)/shard_map/ppermute | solution.py:321
  91.2 23.4 %collective-permute-start.15 = (bf16[640,512]{1,0:T(8,128)(2,1)S(1)}, bf16[640,512]{1,0:T(8,128)(2,1)S(1)}, u32[]{:S(2)}, u32[]{:S(2)}) collective-permute-start(bf16[640,512]{1,0:T(8,128)(2,1)S(1)} %collective-permute-done.12.refs_0_), channel_id=1, source_target_pairs={{0,1},{1,0},{2,3},{3,2},{4,5},{5,4},{6,7},{7,6},{8,9},{9,8},{10,11... | collective-permute-start | bytes 1966088 | tf_op jit(solution)/shard_map/ppermute | solution.py:321
  93.1 21.6 %collective-permute-start.16 = (bf16[4,80,512]{2,1,0:T(8,128)(2,1)}, bf16[4,80,512]{2,1,0:T(8,128)(2,1)S(1)}, u32[]{:S(2)}, u32[]{:S(2)}) collective-permute-start(bf16[4,80,512]{2,1,0:T(8,128)(2,1)} %get-tuple-element.200), channel_id=1, source_target_pairs={{0,1},{1,0},{2,3},{3,2},{4,5},{5,4},{6,7},{7,6},{8,9},{9,8},{10,11... | collective-permute-start | bytes 983048 | tf_op jit(solution)/shard_map/ppermute | solution.py:321
  94.2 20.4 %collective-permute-start.17 = (bf16[4,80,512]{2,1,0:T(8,128)(2,1)S(1)}, bf16[4,80,512]{2,1,0:T(8,128)(2,1)S(1)}, u32[]{:S(2)}, u32[]{:S(2)}) collective-permute-start(bf16[4,80,512]{2,1,0:T(8,128)(2,1)S(1)} %get-tuple-element.198), channel_id=1, source_target_pairs={{0,16},{8,24},{16,0},{24,8},{1,17},{9,25},{17,1},{25,9},{2,18},{10... | collective-permute-start | bytes 983048 | tf_op jit(solution)/shard_map/ppermute | solution.py:321
  115.6 15.6 %collective-permute-start.18 = (bf16[2,4,80,512]{3,2,1,0:T(8,128)(2,1)}, bf16[2,4,80,512]{3,2,1,0:T(8,128)(2,1)S(1)}, u32[]{:S(2)}, u32[]{:S(2)}) collective-permute-start(bf16[2,4,80,512]{3,2,1,0:T(8,128)(2,1)} %get-tuple-element.184), channel_id=1, source_target_pairs={{0,16},{8,24},{16,0},{24,8},{1,17},{9,25},{17,1},{25,9},{2,18},{10... | collective-permute-start | bytes 1966088 | tf_op jit(solution)/shard_map/ppermute | solution.py:321
  117.1 16.3 %collective-permute-start.20 = (bf16[2,4,80,512]{3,2,1,0:T(8,128)(2,1)}, bf16[2,4,80,512]{3,2,1,0:T(8,128)(2,1)S(1)}, u32[]{:S(2)}, u32[]{:S(2)}) collective-permute-start(bf16[2,4,80,512]{3,2,1,0:T(8,128)(2,1)} %get-tuple-element.182), channel_id=1, source_target_pairs={{0,1},{1,0},{2,3},{3,2},{4,5},{5,4},{6,7},{7,6},{8,9},{9,8},{10,11... | collective-permute-start | bytes 1966088 | tf_op jit(solution)/shard_map/ppermute | solution.py:321
  133.3 21.7 %collective-permute-start.19 = (bf16[16,80,512]{2,1,0:T(8,128)(2,1)S(1)}, bf16[16,80,512]{2,1,0:T(8,128)(2,1)}, u32[]{:S(2)}, u32[]{:S(2)}) collective-permute-start(bf16[16,80,512]{2,1,0:T(8,128)(2,1)S(1)} %bitcast.202), channel_id=1, source_target_pairs={{0,8},{8,0},{16,24},{24,16},{1,9},{9,1},{17,25},{25,17},{2,10},{10... | collective-permute-start | bytes 3932168 | tf_op jit(solution)/shard_map/ppermute | solution.py:321
  135.5 19.4 %copy-start.15 = (bf16[2,2,4,80,512]{4,3,2,1,0:T(8,128)(2,1)}, bf16[2,2,4,80,512]{4,3,2,1,0:T(8,128)(2,1)S(1)}, u32[]{:S(2)}) copy-start(bf16[2,2,4,80,512]{4,3,2,1,0:T(8,128)(2,1)S(1)} %pad_maximum_fusion.2) | copy-start | bytes 3932164
  135.5 19.4 %collective-permute-start.21 = (bf16[16,80,512]{2,1,0:T(8,128)(2,1)S(1)}, bf16[16,80,512]{2,1,0:T(8,128)(2,1)}, u32[]{:S(2)}, u32[]{:S(2)}) collective-permute-start(bf16[16,80,512]{2,1,0:T(8,128)(2,1)S(1)} %bitcast.204), channel_id=1, source_target_pairs={{0,8},{8,0},{16,24},{24,16},{1,9},{9,1},{17,25},{25,17},{2,10},{10... | collective-permute-start | bytes 3932168 | tf_op jit(solution)/shard_map/ppermute | solution.py:321
  193.0 8.2 %collective-permute-start.22 = (bf16[2,2,4,176,512]{4,3,2,1,0:T(8,128)(2,1)}, bf16[2,2,4,176,512]{4,3,2,1,0:T(8,128)(2,1)}, u32[]{:S(2)}, u32[]{:S(2)}) collective-permute-start(bf16[2,2,4,176,512]{4,3,2,1,0:T(8,128)(2,1)} %bitcast.241), channel_id=1, source_target_pairs={{0,8},{8,0},{16,24},{24,16},{1,9},{9,1},{17,25},{25,17},{2,10},{10... | collective-permute-start | bytes 8650760 | tf_op jit(solution)/shard_map/ppermute | solution.py:321
  251.8 24.5 %collective-permute-start.35 = (bf16[2,2,4,64,512]{4,3,2,1,0:T(8,128)(2,1)}, bf16[2,2,4,64,512]{4,3,2,1,0:T(8,128)(2,1)}, u32[]{:S(2)}, u32[]{:S(2)}) collective-permute-start(bf16[2,2,4,64,512]{4,3,2,1,0:T(8,128)(2,1)} %bitcast.242), channel_id=1, source_target_pairs={{0,8},{8,0},{16,24},{24,16},{1,9},{9,1},{17,25},{25,17},{2,10},{10... | collective-permute-start | bytes 3145736 | tf_op jit(solution)/shard_map/ppermute | solution.py:321
  252.1 36.4 %collective-permute-start.30 = (bf16[2,4,176,512]{3,2,1,0:T(8,128)(2,1)}, bf16[2,4,176,512]{3,2,1,0:T(8,128)(2,1)}, u32[]{:S(2)}, u32[]{:S(2)}) collective-permute-start(bf16[2,4,176,512]{3,2,1,0:T(8,128)(2,1)} %get-tuple-element.128), channel_id=1, source_target_pairs={{0,16},{8,24},{16,0},{24,8},{1,17},{9,25},{17,1},{25,9},{2,18},{10... | collective-permute-start | bytes 4325384 | tf_op jit(solution)/shard_map/ppermute | solution.py:321
  253.8 105.7 %collective-permute-start.29 = (bf16[512,640]{0,1:T(8,128)(2,1)}, bf16[512,640]{0,1:T(8,128)(2,1)}, u32[]{:S(2)}, u32[]{:S(2)}) collective-permute-start(bf16[512,640]{0,1:T(8,128)(2,1)} %copy.93), channel_id=1, source_target_pairs={{0,1},{1,0},{2,3},{3,2},{4,5},{5,4},{6,7},{7,6},{8,9},{9,8},{10,11... | collective-permute-start | bytes 1966088 | tf_op jit(solution)/shard_map/ppermute | solution.py:321
  256.4 29.4 %collective-permute-start.23 = (bf16[512,640]{0,1:T(8,128)(2,1)}, bf16[512,640]{0,1:T(8,128)(2,1)}, u32[]{:S(2)}, u32[]{:S(2)}) collective-permute-start(bf16[512,640]{0,1:T(8,128)(2,1)} %copy.87), channel_id=1, source_target_pairs={{0,1},{1,0},{2,3},{3,2},{4,5},{5,4},{6,7},{7,6},{8,9},{9,8},{10,11... | collective-permute-start | bytes 1966088 | tf_op jit(solution)/shard_map/ppermute | solution.py:321
  268.6 40.1 %collective-permute-start.25 = (bf16[512,640]{0,1:T(8,128)(2,1)}, bf16[512,640]{0,1:T(8,128)(2,1)}, u32[]{:S(2)}, u32[]{:S(2)}) collective-permute-start(bf16[512,640]{0,1:T(8,128)(2,1)} %copy.89), channel_id=1, source_target_pairs={{0,1},{1,0},{2,3},{3,2},{4,5},{5,4},{6,7},{7,6},{8,9},{9,8},{10,11... | collective-permute-start | bytes 1966088 | tf_op jit(solution)/shard_map/ppermute | solution.py:321
  276.4 69.6 %collective-permute-start.27 = (bf16[512,640]{0,1:T(8,128)(2,1)S(1)}, bf16[512,640]{0,1:T(8,128)(2,1)S(1)}, u32[]{:S(2)}, u32[]{:S(2)}) collective-permute-start(bf16[512,640]{0,1:T(8,128)(2,1)S(1)} %copy-done.27), channel_id=1, source_target_pairs={{0,1},{1,0},{2,3},{3,2},{4,5},{5,4},{6,7},{7,6},{8,9},{9,8},{10,11... | collective-permute-start | bytes 1966088 | tf_op jit(solution)/shard_map/ppermute | solution.py:321
  285.8 11.8 %collective-permute-start.36 = (bf16[2,4,64,512]{3,2,1,0:T(8,128)(2,1)S(1)}, bf16[2,4,64,512]{3,2,1,0:T(8,128)(2,1)S(1)}, u32[]{:S(2)}, u32[]{:S(2)}) collective-permute-start(bf16[2,4,64,512]{3,2,1,0:T(8,128)(2,1)S(1)} %get-tuple-element.168), channel_id=1, source_target_pairs={{0,16},{8,24},{16,0},{24,8},{1,17},{9,25},{17,1},{25,9},{2,18},{10... | collective-permute-start | bytes 1572872 | tf_op jit(solution)/shard_map/ppermute | solution.py:321
  288.5 20.7 %collective-permute-start.24 = (bf16[512,640]{0,1:T(8,128)(2,1)S(1)}, bf16[512,640]{0,1:T(8,128)(2,1)S(1)}, u32[]{:S(2)}, u32[]{:S(2)}) collective-permute-start(bf16[512,640]{0,1:T(8,128)(2,1)S(1)} %add_convert_fusion.8), channel_id=1, source_target_pairs={{0,6},{1,7},{2,0},{3,1},{4,2},{5,3},{6,4},{7,5},{8,14},{9,15},{10,... | collective-permute-start | bytes 1966088 | tf_op jit(solution)/shard_map/ppermute | solution.py:321
  297.9 10.8 %collective-permute-start.37 = (bf16[2,64,512]{2,1,0:T(8,128)(2,1)S(1)}, bf16[2,64,512]{2,1,0:T(8,128)(2,1)S(1)}, u32[]{:S(2)}, u32[]{:S(2)}) collective-permute-start(bf16[2,64,512]{2,1,0:T(8,128)(2,1)S(1)} %pad_maximum_fusion.11), channel_id=1, source_target_pairs={{0,6},{1,7},{2,0},{3,1},{4,2},{5,3},{6,4},{7,5},{8,14},{9,15},{10,... | collective-permute-start | bytes 393224 | tf_op jit(solution)/shard_map/ppermute | solution.py:321
  308.7 16.1 %collective-permute-start.31 = (bf16[2,176,512]{2,1,0:T(8,128)(2,1)S(1)}, bf16[2,176,512]{2,1,0:T(8,128)(2,1)S(1)}, u32[]{:S(2)}, u32[]{:S(2)}) collective-permute-start(bf16[2,176,512]{2,1,0:T(8,128)(2,1)S(1)} %pad_maximum_fusion.7), channel_id=1, source_target_pairs={{0,6},{1,7},{2,0},{3,1},{4,2},{5,3},{6,4},{7,5},{8,14},{9,15},{10,... | collective-permute-start | bytes 1081352 | tf_op jit(solution)/shard_map/ppermute | solution.py:321
  308.7 15.9 %collective-permute-start.38 = (bf16[2,64,512]{2,1,0:T(8,128)(2,1)S(1)}, bf16[2,64,512]{2,1,0:T(8,128)(2,1)S(1)}, u32[]{:S(2)}, u32[]{:S(2)}) collective-permute-start(bf16[2,64,512]{2,1,0:T(8,128)(2,1)S(1)} %add_convert_fusion.18), channel_id=1, source_target_pairs={{0,6},{1,7},{2,0},{3,1},{4,2},{5,3},{6,4},{7,5},{8,14},{9,15},{10,... | collective-permute-start | bytes 393224 | tf_op jit(solution)/shard_map/ppermute | solution.py:321
  310.5 35.5 %collective-permute-start.26 = (bf16[512,640]{0,1:T(8,128)(2,1)S(1)}, bf16[512,640]{0,1:T(8,128)(2,1)S(1)}, u32[]{:S(2)}, u32[]{:S(2)}) collective-permute-start(bf16[512,640]{0,1:T(8,128)(2,1)S(1)} %add_convert_fusion.6), channel_id=1, source_target_pairs={{0,6},{1,7},{2,0},{3,1},{4,2},{5,3},{6,4},{7,5},{8,14},{9,15},{10,... | collective-permute-start | bytes 1966088 | tf_op jit(solution)/shard_map/ppermute | solution.py:321
  324.7 16.8 %collective-permute-start.39 = (bf16[2,64,512]{2,1,0:T(8,128)(2,1)S(1)}, bf16[2,64,512]{2,1,0:T(8,128)(2,1)S(1)}, u32[]{:S(2)}, u32[]{:S(2)}) collective-permute-start(bf16[2,64,512]{2,1,0:T(8,128)(2,1)S(1)} %add_convert_fusion.17), channel_id=1, source_target_pairs={{0,6},{1,7},{2,0},{3,1},{4,2},{5,3},{6,4},{7,5},{8,14},{9,15},{10,... | collective-permute-start | bytes 393224 | tf_op jit(solution)/shard_map/ppermute | solution.py:321
  324.8 21.2 %copy-start.8 = (bf16[512,640]{0,1:T(8,128)(2,1)S(1)}, bf16[512,640]{0,1:T(8,128)(2,1)}, u32[]{:S(2)}) copy-start(bf16[512,640]{0,1:T(8,128)(2,1)} %copy.92) | copy-start | bytes 1966084
  324.9 20.9 %collective-permute-start.32 = (bf16[2,176,512]{2,1,0:T(8,128)(2,1)S(1)}, bf16[2,176,512]{2,1,0:T(8,128)(2,1)S(1)}, u32[]{:S(2)}, u32[]{:S(2)}) collective-permute-start(bf16[2,176,512]{2,1,0:T(8,128)(2,1)S(1)} %add_convert_fusion.13), channel_id=1, source_target_pairs={{0,6},{1,7},{2,0},{3,1},{4,2},{5,3},{6,4},{7,5},{8,14},{9,15},{10,... | collective-permute-start | bytes 1081352 | tf_op jit(solution)/shard_map/ppermute | solution.py:321
  341.6 4.8 %collective-permute-start.40 = (bf16[64,512]{1,0:T(8,128)(2,1)S(1)}, bf16[64,512]{1,0:T(8,128)(2,1)S(1)}, u32[]{:S(2)}, u32[]{:S(2)}) collective-permute-start(bf16[64,512]{1,0:T(8,128)(2,1)S(1)} %slice_bitcast_fusion.23), channel_id=1, source_target_pairs={{0,1},{1,0},{2,3},{3,2},{4,5},{5,4},{6,7},{7,6},{8,9},{9,8},{10,11... | collective-permute-start | bytes 196616 | tf_op jit(solution)/shard_map/ppermute | solution.py:321
  345.9 13.2 %collective-permute-start.33 = (bf16[2,176,512]{2,1,0:T(8,128)(2,1)S(1)}, bf16[2,176,512]{2,1,0:T(8,128)(2,1)S(1)}, u32[]{:S(2)}, u32[]{:S(2)}) collective-permute-start(bf16[2,176,512]{2,1,0:T(8,128)(2,1)S(1)} %add_convert_fusion.12), channel_id=1, source_target_pairs={{0,6},{1,7},{2,0},{3,1},{4,2},{5,3},{6,4},{7,5},{8,14},{9,15},{10,... | collective-permute-start | bytes 1081352 | tf_op jit(solution)/shard_map/ppermute | solution.py:321
  346.3 22.5 %copy-start.7 = (bf16[512,640]{0,1:T(8,128)(2,1)S(1)}, bf16[512,640]{0,1:T(8,128)(2,1)}, u32[]{:S(2)}) copy-start(bf16[512,640]{0,1:T(8,128)(2,1)} %copy.94) | copy-start | bytes 1966084
  346.3 22.5 %copy-start.39 = (f32[1,512]{1,0:T(1,128)S(1)}, f32[1,512]{1,0:T(1,128)}, u32[]{:S(2)}) copy-start(f32[1,512]{1,0:T(1,128)} %get-tuple-element.226) | copy-start | bytes 6148
  346.3 22.5 %collective-permute-start.28 = (bf16[512,640]{0,1:T(8,128)(2,1)S(1)}, bf16[512,640]{0,1:T(8,128)(2,1)S(1)}, u32[]{:S(2)}, u32[]{:S(2)}) collective-permute-start(bf16[512,640]{0,1:T(8,128)(2,1)S(1)} %add_convert_fusion.4), channel_id=1, source_target_pairs={{0,6},{1,7},{2,0},{3,1},{4,2},{5,3},{6,4},{7,5},{8,14},{9,15},{10,... | collective-permute-start | bytes 1966088 | tf_op jit(solution)/shard_map/ppermute | solution.py:321
  359.2 13.3 %collective-permute-start.34 = (bf16[176,512]{1,0:T(8,128)(2,1)S(1)}, bf16[176,512]{1,0:T(8,128)(2,1)S(1)}, u32[]{:S(2)}, u32[]{:S(2)}) collective-permute-start(bf16[176,512]{1,0:T(8,128)(2,1)S(1)} %slice_bitcast_fusion.5), channel_id=1, source_target_pairs={{0,1},{1,0},{2,3},{3,2},{4,5},{5,4},{6,7},{7,6},{8,9},{9,8},{10,11... | collective-permute-start | bytes 540680 | tf_op jit(solution)/shard_map/ppermute | solution.py:321
  (40 other events, 170.2 us)
